TPU v7x, 32 devices: a whole 2x2x4 slice. The times are simulated.
32 devices in a mesh: rep: 4 (over x, core), fsdp: 8 (over z, y).
Axes of the slice: x: 2, y: 2, z: 4, core: 2. Of those that a mesh axis runs over, the one named last changes fastest.
Arguments:
- tokens: bfloat16 [45312, 768], P(('rep', 'fsdp')), may hold values from -6 to 6
- lengths: int32 [124], replicated, may hold values from 196 to 1024, as said below
- assign: int32 [124], replicated, may hold values from 0 to 31, as said below
- w_in: bfloat16 [768, 5376], P('fsdp'), may hold values from -0.21875 to 0.21875
- w_out: bfloat16 [3840, 768], P('fsdp')
- ln_scale: bfloat16 [768], P('fsdp'), may hold values from 0.5 to 1.5
- q_scale: bfloat16 [64], P('fsdp'), may hold values from 1 to 2
- k_scale: bfloat16 [64], P('fsdp'), may hold values from 1 to 2
- mlp_bias: bfloat16 [3072], P('fsdp'), may hold values from -3 to 3
- out_bias: bfloat16 [768], P('fsdp'), may hold values from -3 to 3
- cotangent: bfloat16 [45312, 768], P(('rep', 'fsdp')), may hold values from -6 to 6
Outputs:
- output: bfloat16 [45312, 768], P(('rep', 'fsdp'))
- grad_tokens: bfloat16 [45312, 768], P(('rep', 'fsdp'))
- grad_w_in: float32 [768, 5376], P('fsdp')
- grad_w_out: float32 [3840, 768], P('fsdp')
- grad_ln_scale: float32 [768], P('fsdp')
- grad_q_scale: float32 [64], P('fsdp')
- grad_k_scale: float32 [64], P('fsdp')
- grad_mlp_bias: float32 [3072], P('fsdp')
- grad_out_bias: float32 [768], P('fsdp')
Inputs may be any that keep to these rules, and one draw needn't show every extreme that they name: `lengths`: each image has 196 or 1024 tokens. `assign`: in each aligned group of eight devices one holds one image of 1024 tokens and two of 196 (1416 tokens), and the seven others hold 1, 2, 3, 4, 5, 6 and 7 images of 196 tokens; no device holds more than 1416 tokens.
All inputs are finite; a program needn't handle non-finite values.
Results may differ from a plain program's by a relative error of at most 0.012.
The roundings to bfloat16 on the way count: a program that leaves them out, or rounds other values in their place, can miss the bound.
Values may be sent and summed in bfloat16 or wider, within the bound.
No kernel may reach another device: no remote copies, remote signals or barrier semaphores. Data moves between devices by JAX's collectives and lax.ppermute only.
A program may use at most 320 MiB of HBM per device.

v0:
```python
import jax
import jax.numpy as jnp
from jax import lax
from jax.sharding import PartitionSpec as P

HEADS = 12
HD = 64


epsilon = 1e-06


def layer_norm(values, weight_gain):
    center = values - jnp.mean(values, axis=-1, keepdims=True)
    spread = jnp.mean(center * center, axis=-1, keepdims=True)
    return center * lax.rsqrt(spread + epsilon) * weight_gain


def layout(lengths, assign, device, row_count):
    own = assign == device
    own_sizes = jnp.where(own, lengths, 0)
    own_ends = jnp.cumsum(own_sizes)
    own_starts = own_ends - own_sizes
    position = lax.broadcasted_iota(jnp.int32, (row_count, lengths.shape[0]), 0)
    number = lax.broadcasted_iota(jnp.int32, (row_count, lengths.shape[0]), 1)
    inside = (position >= own_starts[None, :]) & (position < own_ends[None, :])
    filled = jnp.any(inside, axis=1)
    segment = jnp.sum(jnp.where(inside, number, 0), axis=1)
    return (jnp.where(filled, segment, -1), filled)


def contract_rows(left, right):
    return lax.dot_general(
        left, right, (((0,), (0,)), ((), ())), preferred_element_type=jnp.float32
    )


def contract_cols(left, right):
    return lax.dot_general(
        left, right, (((1,), (1,)), ((), ())), preferred_element_type=jnp.float32
    )


def per_device(
    tokens, lengths, assign, w_in, w_out, ln_scale, q_scale, k_scale, mlp_bias, out_bias, cotangent
):
    row_count = tokens.shape[0]
    head_dim = HD
    head_count = HEADS
    width = head_dim * head_count
    factor = head_dim ** (-0.5)
    device = lax.axis_index("rep") * lax.axis_size("fsdp") + lax.axis_index("fsdp")
    segment, filled = layout(lengths, assign, device, row_count)
    allowed = segment[:, None] == segment[None, :]
    params = (w_in, w_out, ln_scale, q_scale, k_scale, mlp_bias, out_bias)
    full = (
        lax.all_gather(params[0], "fsdp", axis=0, tiled=True),
        lax.all_gather(params[1], "fsdp", axis=0, tiled=True),
        lax.all_gather(params[2], "fsdp", axis=0, tiled=True),
        lax.all_gather(params[3], "fsdp", axis=0, tiled=True),
        lax.all_gather(params[4], "fsdp", axis=0, tiled=True),
        lax.all_gather(params[5], "fsdp", axis=0, tiled=True),
        lax.all_gather(params[6], "fsdp", axis=0, tiled=True),
    )
    win_full, wout_full = (full[0], full[1])
    small = [arr.astype(jnp.float32) for arr in full[2:]]
    ln_full, qs_full, ks_full, mb_full, ob_full = small
    inputs = tokens.astype(jnp.float32)
    normed_f, ln_pull = jax.vjp(layer_norm, inputs, ln_full)
    normed = normed_f.astype(jnp.bfloat16)
    joined = jnp.dot(normed, win_full, preferred_element_type=jnp.float32)
    q_pre = joined[:, :width].reshape(row_count, head_count, head_dim)
    k_pre = joined[:, width : 2 * width].reshape(row_count, head_count, head_dim)
    values = joined[:, 2 * width : 3 * width].astype(jnp.bfloat16)
    hidden_pre = joined[:, 3 * width :]
    q_norm, q_pull = jax.vjp(layer_norm, q_pre, qs_full)
    k_norm, k_pull = jax.vjp(layer_norm, k_pre, ks_full)
    queries = q_norm.reshape(row_count, width).astype(jnp.bfloat16)
    keys_all = k_norm.reshape(row_count, width).astype(jnp.bfloat16)

    def head_slice(array, head_index):
        return lax.dynamic_slice_in_dim(array, head_index * head_dim, head_dim, 1)

    def head_scores(head_index):
        raw = (
            contract_cols(head_slice(queries, head_index), head_slice(keys_all, head_index))
            * factor
        )
        return jnp.where(allowed, raw, -1e30)

    def head_forward(head_index):
        scores = head_scores(head_index)
        top = jnp.max(scores, axis=1, keepdims=True)
        expon = jnp.exp(scores - top)
        total = jnp.sum(expon, axis=1, keepdims=True)
        probs = (expon / total).astype(jnp.bfloat16)
        head_out = jnp.dot(
            probs, head_slice(values, head_index), preferred_element_type=jnp.float32
        )
        return (head_out, (top + jnp.log(total))[:, 0])

    head_outs, log_totals = lax.map(head_forward, jnp.arange(head_count))
    attended = jnp.transpose(head_outs, (1, 0, 2)).reshape(row_count, width)
    activated, gelu_pull = jax.vjp(lambda pre, bias: jax.nn.gelu(pre + bias), hidden_pre, mb_full)
    merged = jnp.concatenate([attended, activated], axis=1).astype(jnp.bfloat16)
    result = jnp.dot(merged, wout_full, preferred_element_type=jnp.float32) + ob_full
    output = jnp.where(filled[:, None], inputs + result, 0.0).astype(jnp.bfloat16)
    back = (
        lax.all_gather(params[0], "fsdp", axis=0, tiled=True),
        lax.all_gather(params[1], "fsdp", axis=0, tiled=True),
        lax.all_gather(params[2], "fsdp", axis=0, tiled=True),
        lax.all_gather(params[3], "fsdp", axis=0, tiled=True),
        lax.all_gather(params[4], "fsdp", axis=0, tiled=True),
        lax.all_gather(params[5], "fsdp", axis=0, tiled=True),
        lax.all_gather(params[6], "fsdp", axis=0, tiled=True),
    )
    win_back, wout_back = (back[0], back[1])
    grad_rows = jnp.where(filled[:, None], cotangent.astype(jnp.float32), 0.0)
    grad_low = grad_rows.astype(jnp.bfloat16)
    grad_ob = jnp.sum(grad_rows, axis=0)
    grad_wout = contract_rows(merged, grad_low)
    grad_merged = contract_cols(grad_low, wout_back)
    grad_attended = grad_merged[:, :width].astype(jnp.bfloat16)
    grad_m, grad_mb = gelu_pull(grad_merged[:, width:])

    def head_backward(head_index):
        scores = head_scores(head_index)
        probs_full = jnp.exp(scores - log_totals[head_index][:, None])
        probs = probs_full.astype(jnp.bfloat16)
        grad_head = head_slice(grad_attended, head_index)
        grad_probs = contract_cols(grad_head, head_slice(values, head_index))
        inner = jnp.sum(probs_full * grad_probs, axis=1, keepdims=True)
        grad_scores = (probs_full * (grad_probs - inner)).astype(jnp.bfloat16)
        grad_q = (
            jnp.dot(
                grad_scores, head_slice(keys_all, head_index), preferred_element_type=jnp.float32
            )
            * factor
        )
        grad_k = contract_rows(grad_scores, head_slice(queries, head_index)) * factor
        grad_v = contract_rows(probs, grad_head)
        return (grad_q, grad_k, grad_v)

    grad_qh, grad_kh, grad_vh = lax.map(head_backward, jnp.arange(head_count))
    grad_qn = jnp.transpose(grad_qh, (1, 0, 2))
    grad_kn = jnp.transpose(grad_kh, (1, 0, 2))
    grad_values = jnp.transpose(grad_vh, (1, 0, 2)).reshape(row_count, width)
    grad_q_pre, grad_qs = q_pull(grad_qn)
    grad_k_pre, grad_ks = k_pull(grad_kn)
    grad_joined = jnp.concatenate(
        [
            grad_q_pre.reshape(row_count, width),
            grad_k_pre.reshape(row_count, width),
            grad_values,
            grad_m,
        ],
        axis=1,
    ).astype(jnp.bfloat16)
    grad_win = contract_rows(normed, grad_joined)
    grad_normed = contract_cols(grad_joined, win_back)
    grad_x_norm, grad_ln = ln_pull(grad_normed)
    grad_tokens = (grad_rows + grad_x_norm).astype(jnp.bfloat16)
    grads = (grad_win, grad_wout, grad_ln, grad_qs, grad_ks, grad_mb, grad_ob)
    shares = (
        lax.psum_scatter(grads[0], "fsdp", scatter_dimension=0, tiled=True),
        lax.psum_scatter(grads[1], "fsdp", scatter_dimension=0, tiled=True),
        lax.psum_scatter(grads[2], "fsdp", scatter_dimension=0, tiled=True),
        lax.psum_scatter(grads[3], "fsdp", scatter_dimension=0, tiled=True),
        lax.psum_scatter(grads[4], "fsdp", scatter_dimension=0, tiled=True),
        lax.psum_scatter(grads[5], "fsdp", scatter_dimension=0, tiled=True),
        lax.psum_scatter(grads[6], "fsdp", scatter_dimension=0, tiled=True),
    )
    shares = lax.psum(
        (shares[0], shares[1], shares[2], shares[3], shares[4], shares[5], shares[6]), "rep"
    )
    return (
        output,
        grad_tokens,
        shares[0],
        shares[1],
        shares[2],
        shares[3],
        shares[4],
        shares[5],
        shares[6],
    )


def solution(mesh):
    in_specs = (
        P(("rep", "fsdp"), None),
        P(),
        P(),
        P("fsdp", None),
        P("fsdp", None),
        P("fsdp"),
        P("fsdp"),
        P("fsdp"),
        P("fsdp"),
        P("fsdp"),
        P(("rep", "fsdp"), None),
    )
    out_specs = (
        P(("rep", "fsdp"), None),
        P(("rep", "fsdp"), None),
        P("fsdp", None),
        P("fsdp", None),
        P("fsdp"),
        P("fsdp"),
        P("fsdp"),
        P("fsdp"),
        P("fsdp"),
    )
    return jax.shard_map(
        per_device, mesh=mesh, in_specs=in_specs, out_specs=out_specs, check_vma=False
    )
```

profile of v0, /device:TPU:0, one launch (start us, length us, event | category | flops | bytes accessed | tf_op | source)
XLA Modules:
  0.0 1304.4 jit_solution(14845340420748223107)
XLA Ops:
  15.5 24.7 %all-reduce.12 = (bf16[768]{0:T(1024)(128)(2,1)S(1)}, bf16[64]{0:T(256)(128)(2,1)S(1)}, bf16[64]{0:T(256)(128)(2,1)S(1)}, bf16[768]{0:T(1024)(128)(2,1)}) all-reduce(bf16[768]{0:T(1024)(128)(2,1)S(1)} %dynamic-update-slice, bf16[64]{0:T(256)(128)(2,1)S(1)} %dynamic-update-slice.1, ...), channel_id=1, replica_groups=mesh['rep'=4,'fsdp'=8] {'fsdp'}, use_global_device_ids=true, to_apply=%add | all-reduce | flops 1664 | bytes 6656
  41.4 26.3 %all-gather = bf16[8,1,384]{2,1,0:T(2,128)(2,1)S(1)} all-gather(bf16[1,1,384]{2,1,0:T(2,128)(2,1)S(1)} %reshape.219), channel_id=1, replica_groups=mesh['rep'=4,'fsdp'=8] {'fsdp'}, dimensions={0}, use_global_device_ids=true | all-gather | bytes 6912 | tf_op jit(solution)/shard_map/all_gather | solution.py:62
  74.2 33.6 %all-gather.6.cloned.1.call-done = bf16[3840,768]{1,0:T(8,128)(2,1)} async-done(((bf16[480,768]{1,0:T(8,128)(2,1)}), bf16[3840,768]{1,0:T(8,128)(2,1)}) %all-gather.6.cloned.1.call-update) | async-done | bytes 5898256 | tf_op jit(solution)/shard_map/all_gather | solution.py:58
  107.9 16.4 %fusion.69 = f32[1416,3840]{1,0:T(8,128)} fusion(bf16[3840,768]{1,0:T(8,128)(2,1)} %all-gather.6.cloned.1.call-done, bf16[1416,768]{1,0:T(8,128)(2,1)} %param.25, pred[1416]{0:T(1024)(128)(4,1)S(1)} %fusion.72), kind=kOutput, calls=%fused_computation.100 | convolution fusion | flops 8355170304 | bytes 29824392 | tf_op jit(solution)/shard_map/dot_general | solution.py:39
  128.1 103.4 %all-gather.4.cloned.1.call-done = bf16[768,5376]{1,0:T(8,128)(2,1)} async-done(((bf16[96,5376]{1,0:T(8,128)(2,1)}), bf16[768,5376]{1,0:T(8,128)(2,1)}) %all-gather.4.cloned.1.call-update) | async-done | bytes 8257552 | tf_op jit(solution)/shard_map/all_gather | solution.py:57
  231.5 20.1 %fusion.87 = f32[1416,5376]{1,0:T(8,128)} fusion(bf16[768,5376]{1,0:T(8,128)(2,1)} %all-gather.4.cloned.1.call-done, bf16[1416,768]{1,0:T(8,128)(2,1)S(1)} %copy-done.3, f32[768]{0:T(1024)S(1)} %convert_element_type.53, f32[1416]{0:T(1024)S(1)} %fusion.75, f32[1416]{0:T(1024)S(1)} %broadcast_multiply_fusion.2), kind=kOutput, calls=%fused_computation.133 | convolution fusion | flops 11698108416 | bytes 40896576 | tf_op jit(solution)/shard_map/dot_general | solution.py:71
  255.4 7.6 fusion.93
  263.0 24.5 %fusion.90 = (f32[3072]{0:T(1024)}, bf16[1416,3072]{1,0:T(8,128)(2,1)}, bf16[1416,3072]{1,0:T(8,128)(2,1)}) fusion(f32[3072]{0:T(1024)S(1)} %bitcast.116, f32[1416,5376]{1,0:T(8,128)} %fusion.87, f32[1416,3840]{1,0:T(8,128)} %fusion.69), kind=kLoop, calls=%fused_computation.135 | loop fusion | flops 104395776 | bytes 52224000 | tf_op jit(solution)/shard_map/transpose(jvp())/reduce_sum | solution.py:104
  287.4 6.3 copy.57
  302.5 5.9 copy.59
  311.1 5.9 copy.58
  317.0 5.9 copy.54
  331.6 5.9 copy.56
  340.3 5.9 copy.55
  346.2 11.5 multiply_convert_fusion.2
  357.7 101.3 %while.30 = (s32[]{:T(128)}, bf16[12,1416,64]{1,2,0:T(8,128)(2,1)S(1)}, f32[12,1416]{1,0:T(8,128)S(1)}, s32[12]{0:T(128)S(1)}, bf16[1416,768]{1,0:T(8,128)(2,1)}...) while((s32[]{:T(128)}, ...), condition=%wide.region_12.13_spmd.clone.clone, body=%wide.region_9.12_spmd.clone.sunk.clone | while | flops 531338432 | bytes 26311660 | solution.py:102
  461.5 16.6 %fusion.48 = f32[3840,768]{1,0:T(8,128)} fusion(bf16[1416,3072]{1,0:T(8,128)(2,1)} %get-tuple-element.226, bf16[1416,768]{1,0:T(8,128)(2,1)} %copy.60, bf16[1416,768]{1,0:T(8,128)(2,1)} %param.25, pred[1416]{0:T(1024)(128)(4,1)S(1)} %copy-done.32), kind=kOutput, calls=%fused_computation.60 | convolution fusion | flops 8376920064 | bytes 24847752 | tf_op jit(solution)/shard_map/dot_general | solution.py:33
  478.2 402.1 %while.31 = (s32[]{:T(128)}, f32[12,1416,64]{1,2,0:T(8,128)}, f32[12,1416,64]{1,2,0:T(8,128)}, bf16[12,1416,64]{1,2,0:T(8,128)(2,1)}, s32[12]{0:T(128)S(1)}, /*i...) while((s32[]{:T(128)}, f32[12,1416,64]{1,2,0:T(8,128)}, ...), condition=%wide.region_15.16_spmd.clone.clone, body=%wide.region_13.15_spmd.clone.sunk.clone | while | flops 1303466240 | bytes 97358600 | solution.py:144
  483.9 7.8 multiply_reduce_fusion.7
  491.8 8.3 multiply_convert_fusion.6
  500.1 5.7 fusion.149
  517.5 7.8 multiply_reduce_fusion.7
  525.3 8.5 multiply_convert_fusion.6
  533.8 6.0 fusion.149
  551.5 7.8 multiply_reduce_fusion.7
  559.3 8.4 multiply_convert_fusion.6
  567.8 5.6 fusion.149
  585.1 7.8 multiply_reduce_fusion.7
  592.9 8.7 multiply_convert_fusion.6
  601.6 5.6 fusion.149
  618.9 7.9 multiply_reduce_fusion.7
  626.8 8.3 multiply_convert_fusion.6
  635.1 5.7 fusion.149
  652.5 7.8 multiply_reduce_fusion.7
  660.3 8.3 multiply_convert_fusion.6
  668.6 5.6 fusion.149
  685.9 7.8 multiply_reduce_fusion.7
  693.8 8.2 multiply_convert_fusion.6
  702.0 5.6 fusion.149
  719.3 7.8 multiply_reduce_fusion.7
  727.1 8.2 multiply_convert_fusion.6
  735.3 5.6 fusion.149
  752.6 7.8 multiply_reduce_fusion.7
  760.4 8.2 multiply_convert_fusion.6
  768.6 5.6 fusion.149
  785.9 7.8 multiply_reduce_fusion.7
  793.7 8.2 multiply_convert_fusion.6
  801.9 5.6 fusion.149
  819.3 7.8 multiply_reduce_fusion.7
  827.1 8.2 multiply_convert_fusion.6
  835.3 5.6 fusion.149
  852.6 7.8 multiply_reduce_fusion.7
  860.5 8.2 multiply_convert_fusion.6
  868.7 5.6 fusion.149
  884.9 5.3 multiply_reduce_fusion.2
  895.8 4.7 fusion.56
  904.5 6.8 add_convert_fusion.1
  915.8 24.6 %fusion.66 = f32[768,5376]{1,0:T(8,128)} fusion(bf16[1416,3072]{1,0:T(8,128)(2,1)} %get-tuple-element.221, bf16[1416,768]{1,0:T(8,128)(2,1)} %copy.63, bf16[1416,768]{1,0:T(8,128)(2,1)} %copy.62, bf16[1416,768]{1,0:T(8,128)(2,1)} %copy.61, bf16[1416,768]{1,0:T(8,128)(2,1)S(1)} %copy-done.4, f32[768]{0:T(1024)S(1)} %copy-done.30, f32[1416]{0:T(1024)S(1)} %copy-done.27, ...), kind=kOutput, calls=%fused_computation.98 | convolution fusion | flops 11759007744 | bytes 33929280 | tf_op jit(solution)/shard_map/dot_general | solution.py:33
  942.4 20.6 %fusion.61 = (f32[1416]{0:T(1024)S(1)}, f32[1416,768]{1,0:T(8,128)}) fusion(bf16[1416,768]{1,0:T(8,128)(2,1)S(1)} %copy-done.4, f32[768]{0:T(1024)S(1)} %copy-done.30, f32[1416]{0:T(1024)S(1)} %copy-done.23, bf16[768,5376]{1,0:T(8,128)(2,1)} %all-gather.4.cloned.1.call-done, bf16[1416,3072]{1,0:T(8,128)(2,1)} %get-tuple-element.221, ...), kind=kOutput, calls=%fused_computation.87 | convolution fusion | flops 11759006720 | bytes 30021696 | tf_op jit(solution)/shard_map/dot_general | solution.py:39
  970.7 35.9 %all-reduce.9 = (f32[768]{0:T(1024)S(1)}, f32[64]{0:T(128)S(1)}, f32[64]{0:T(128)S(1)}, f32[3072]{0:T(1024)S(1)}, f32[768]{0:T(1024)S(1)}) all-reduce(f32[768]{0:T(1024)S(1)} %get-tuple-element.164, f32[64]{0:T(128)S(1)} %get-tuple-element.240, f32[64]{0:T(128)S(1)} %get-tuple-element.160, ...), channel_id=4, replica_groups=mesh['rep'=4,'fsdp'=8] {'fsdp'}, use_global_device_ids=true, to_apply=%region_27.28.clone | all-reduce | flops 4736 | bytes 37888
  1007.0 6.6 all-reduce.10
  1013.6 203.2 %reduce-scatter.3.cloned.1.call-done = f32[96,5376]{1,0:T(8,128)} async-done(((f32[768,5376]{1,0:T(8,128)}), f32[96,5376]{1,0:T(8,128)}) %reduce-scatter.3.cloned.1.call-update) | async-done | bytes 2064400 | tf_op jit(solution)/shard_map/reduce_scatter | solution.py:165
  1216.8 14.3 %fusion.63 = bf16[1416,768]{1,0:T(8,128)(2,1)} fusion(bf16[1416,768]{1,0:T(8,128)(2,1)S(1)} %copy-done.4, bf16[3840,768]{1,0:T(8,128)(2,1)} %all-gather.6.cloned.1.call-done, bf16[1416,3072]{1,0:T(8,128)(2,1)} %get-tuple-element.226, bf16[1416,768]{1,0:T(8,128)(2,1)} %copy.60, f32[768]{0:T(1024)S(1)} %convert_element_type.60, pred[1416]{0:T(1024)(128)(4,1)S(1)} %copy-done.33), kind=kOutput, calls=%fused_computation.89 | convolution fusion | flops 8379095040 | bytes 21127560 | tf_op jit(solution)/shard_map/dot_general | solution.py:106
  1231.2 62.2 %all-reduce.15.cloned.1.call-done = (f32[96,5376]{1,0:T(8,128)}, f32[480,768]{1,0:T(8,128)}) async-done(((f32[96,5376]{1,0:T(8,128)}, f32[480,768]{1,0:T(8,128)}), (f32[96,5376]{1,0:T(8,128)}, f32[480,768]{1,0:T(8,128)})) %all-reduce.15.cloned.1.call-update) | async-done | bytes 3538960 | tf_op jit(solution)/shard_map/psum | solution.py:173
  (338 shorter events, 281.0 us)
Async XLA Ops:
  7.2 64.7 %copy-start.38 = (s32[124]{0:T(128)S(1)}, s32[124]{0:T(128)}, u32[]{:S(2)}) copy-start(s32[124]{0:T(128)} %param.17) | copy-start | bytes 1492
  7.2 64.7 %copy-start.37 = (s32[124]{0:T(128)S(1)}, s32[124]{0:T(128)}, u32[]{:S(2)}) copy-start(s32[124]{0:T(128)} %param.16) | copy-start | bytes 1492
  7.2 65.3 %copy-start.3 = (bf16[1416,768]{1,0:T(8,128)(2,1)S(1)}, bf16[1416,768]{1,0:T(8,128)(2,1)}, u32[]{:S(2)}) copy-start(bf16[1416,768]{1,0:T(8,128)(2,1)} %param.15) | copy-start | bytes 6524932
  7.2 100.7 %all-gather.6.cloned.1.call-start = ((), (), s32[]{:S(2)}) async-start(), calls=%async_computation.3 | async-start | bytes 6635520 | tf_op jit(solution)/shard_map/all_gather | solution.py:58
  7.9 223.5 %all-gather.4.cloned.1.call-start = ((), (), s32[]{:S(2)}) async-start(), calls=%async_computation.2 | async-start | bytes 9289728 | tf_op jit(solution)/shard_map/all_gather | solution.py:57
  8.7 1004.9 %reduce-scatter.5.cloned.1.call-start = ((), (), s32[]{:S(2)}) async-start(), calls=%async_computation.5 | async-start | bytes 13271040 | tf_op jit(solution)/shard_map/reduce_scatter | solution.py:166
  41.2 190.3 %copy-start.29 = (f32[768]{0:T(1024)}, f32[768]{0:T(1024)S(1)}, u32[]{:S(2)}) copy-start(f32[768]{0:T(1024)S(1)} %convert_element_type.53) | copy-start | bytes 9220
  69.0 1.4 copy-start.5
  72.2 52.1 %copy-start.31 = (pred[1416]{0:T(1024)(128)(4,1)}, pred[1416]{0:T(1024)(128)(4,1)S(1)}, u32[]{:S(2)}) copy-start(pred[1416]{0:T(1024)(128)(4,1)S(1)} %fusion.72) | copy-start | bytes 4252
  72.8 158.6 %copy-start.22 = (f32[1416]{0:T(1024)}, f32[1416]{0:T(1024)S(1)}, u32[]{:S(2)}) copy-start(f32[1416]{0:T(1024)S(1)} %broadcast_multiply_fusion.2) | copy-start | bytes 16996
  73.6 0.6 copy-start.24
  74.2 157.2 %copy-start.26 = (f32[1416]{0:T(1024)}, f32[1416]{0:T(1024)S(1)}, u32[]{:S(2)}) copy-start(f32[1416]{0:T(1024)S(1)} %fusion.75) | copy-start | bytes 16996
  296.6 11.8 copy-start.8
  299.7 8.7 copy-start.18
  299.8 8.6 copy-start.13
  325.8 11.8 copy-start.10
  328.9 8.7 copy-start.20
  328.9 8.6 copy-start.15
  346.2 11.5 copy-start.7
  357.6 103.8 %copy-start.32 = (pred[1416]{0:T(1024)(128)(4,1)S(1)}, pred[1416]{0:T(1024)(128)(4,1)}, u32[]{:S(2)}) copy-start(pred[1416]{0:T(1024)(128)(4,1)} %copy-done.31) | copy-start | bytes 4252
  478.1 738.7 %reduce-scatter.3.cloned.1.call-start = ((), (), s32[]{:S(2)}) async-start(), calls=%async_computation.4 | async-start | bytes 18579456 | tf_op jit(solution)/shard_map/reduce_scatter | solution.py:165
  478.2 406.7 %copy-start.11 = (f32[1416,12]{0,1:T(8,128)S(1)}, f32[1416,12]{0,1:T(8,128)}, u32[]{:S(2)}) copy-start(f32[1416,12]{0,1:T(8,128)} %copy-done.10) | copy-start | bytes 203908
  478.2 406.7 %copy-start.34 = (f32[64]{0:T(128)S(1)}, f32[64]{0:T(128)}, u32[]{:S(2)}) copy-start(f32[64]{0:T(128)} %convert_element_type.55) | copy-start | bytes 772
  483.9 7.9 copy-start
  517.4 7.8 copy-start
  551.5 7.9 copy-start
  585.1 7.8 copy-start
  618.9 7.9 copy-start
  652.5 7.8 copy-start
  685.9 7.8 copy-start
  719.3 7.8 copy-start
  752.6 7.8 copy-start
  785.9 7.8 copy-start
  819.3 7.8 copy-start
  852.6 7.8 copy-start
  884.8 5.4 copy-start.21
  884.8 5.4 copy-start.1
  884.9 5.4 copy-start.9
  884.9 5.4 copy-start.35
  884.9 9.4 copy-start.19
  884.9 9.4 slice-start
  890.2 4.1 slice-start.2
  890.3 4.1 slice-start.1
  890.3 4.1 slice-start.3
  890.3 5.5 copy-start.2
  890.3 5.5 copy-start.14
  890.4 5.5 copy-start.16
  904.4 11.3 copy-start.4
  904.5 11.3 copy-start.23
  904.5 11.3 copy-start.27
  904.5 11.3 copy-start.30
  940.4 2.0 copy-start.36
  940.4 353.0 %all-reduce.15.cloned.1.call-start = ((), (), s32[]{:S(2)}) async-start(), calls=%async_computation.6 | async-start | bytes 7077888 | tf_op jit(solution)/shard_map/psum | solution.py:173
  942.4 20.6 %copy-start.25 = (f32[1416]{0:T(1024)S(1)}, f32[1416]{0:T(1024)}, u32[]{:S(2)}) copy-start(f32[1416]{0:T(1024)} %copy-done.24) | copy-start | bytes 16996
  963.0 4.5 copy-start.6
  963.0 4.5 copy-start.12
  963.0 4.5 copy-start.33
  967.5 3.3 copy-start.28
  1293.4 3.1 copy-start.17
Sparse Core Ops, SparseCore 0:
  10.2 97.5 all-gather.5
  110.1 121.3 all-gather.3
  478.2 194.3 reduce-scatter.4
  940.5 276.2 reduce-scatter.2
  1219.3 73.9 all-reduce.14
where the time goes:
time: 1310 us; the launch traced here: 1300 us
  matrix products  445 us (34%)
  waiting for transfers between devices  404 us (31%)
  other arithmetic  197 us (15%)
  local copies, waits for them, and re-layouts  108 us (8%)
  blocking collectives  93.5 us (7%)
  loops' own time  39 us (3%)
  between operations  18 us (1%)
    reduce_scatter x1, waiting for transfers between devices, per_device(): lax.psum_scatter(grads[0], 'fsdp', scatter_dimension=0, tiled=True)  203 us
    dot_general x38, matrix products, contract_cols(): lax.dot_general(left, right, (((1,), (1,)), ((), ())), preferred_element_...  198 us
    dot_general x26, matrix products, contract_rows(): lax.dot_general(left, right, (((0,), (0,)), ((), ())), preferred_element_...  148 us
    all_gather x1, waiting for transfers between devices, per_device(): lax.all_gather(params[0], 'fsdp', axis=0, tiled=True)  103 us
    convert_element_type x12, other arithmetic, head_backward(): grad_scores = (probs_full * (grad_probs - inner)).astype(jnp.bfloat16)  99.8 us
    psum x1, waiting for transfers between devices, per_device(): lax.psum((shares[0], shares[1], shares[2], shares[3], shares[4], shares[5...  62.2 us
    unnamed x2, blocking collectives  60.6 us
    all_gather x1, waiting for transfers between devices, per_device(): lax.all_gather(params[1], 'fsdp', axis=0, tiled=True)  33.6 us
  transfers between devices with their start and end apart: 5, of which 4 were waited for; matrix products, arithmetic and copies ran while one was open for 39% of the time, Pallas kernels for 0%

commit v1 on v0

--- a/solution.py
+++ b/solution.py
@@ -1,12 +1,705 @@
+import functools
+
 import jax
 import jax.numpy as jnp
 from jax import lax
+from jax.experimental import pallas as pl
+from jax.experimental.pallas import tpu as pltpu
 from jax.sharding import PartitionSpec as P
 
+D = 768
+HD = 64
+SMALL = 196
+BIG = 1024
+BLK = 208
+CAN = 7 * BLK
+ROWS = 3072
+RB = 512
+NRB = ROWS // RB
+U = 512
+EPS = 1e-06
+BF = jnp.bfloat16
+F32 = jnp.float32
+VLIM = 60 * 1024 * 1024
+ANYWHERE = pl.BlockSpec(memory_space=pltpu.VMEM)
+SCALARS = pl.BlockSpec(memory_space=pltpu.SMEM)
+
+
+def dot_nn(a, b):
+    return lax.dot_general(a, b, (((1,), (0,)), ((), ())), preferred_element_type=F32)
+
+
+def dot_nt(a, b):
+    return lax.dot_general(a, b, (((1,), (1,)), ((), ())), preferred_element_type=F32)
+
+
+def dot_tn(a, b):
+    return lax.dot_general(a, b, (((0,), (0,)), ((), ())), preferred_element_type=F32)
+
+
+def two_parts(x):
+    hi = x.astype(BF)
+    return hi, (x - hi.astype(F32)).astype(BF)
+
+
+def call(body, out_shape, scratch, args, in_specs, out_specs=None, grid=None, prefetch=0, cost=None):
+    params = pltpu.CompilerParams(vmem_limit_bytes=VLIM)
+    if out_specs is None:
+        out_specs = jax.tree.map(lambda _: ANYWHERE, out_shape)
+    spec = pltpu.PrefetchScalarGridSpec(
+        num_scalar_prefetch=prefetch,
+        grid=grid or (),
+        in_specs=in_specs,
+        out_specs=out_specs,
+        scratch_shapes=scratch,
+    )
+    estimate = None if cost is None else pl.CostEstimate(flops=cost[0], bytes_accessed=cost[1], transcendentals=0)
+    return pl.pallas_call(body, grid_spec=spec, out_shape=out_shape, compiler_params=params, cost_estimate=estimate)(*args)
+
+
+def head_mean_matrix(scale):
+    row = lax.broadcasted_iota(jnp.int32, (256, 128), 0)
+    col = lax.broadcasted_iota(jnp.int32, (256, 128), 1)
+    same = (row // HD) % 2 == col // HD
+    return jnp.where(same, scale, 0.0).astype(BF)
+
+
+def per_head(x, matrix):
+    hi, lo = two_parts(x)
+    return dot_nn(jnp.concatenate([hi, lo], axis=1), matrix)
+
+
+def attention_body(info, nrm, cot, wqkv, wo, gq, gk, att_o, dqkv_o, dw_o, dwo_o, dgq_o, dgk_o,
+                   qa, kb, vv, qp, do, xq, xk, rq, rk, dq, dk, dv, dw, dwo, dg):
+    nb = info[0]
+    lane = lax.broadcasted_iota(jnp.int32, (1, 128), 1)
+    first = lane < HD
+    mean_m = head_mean_matrix(1.0 / HD)
+    sum_m = head_mean_matrix(1.0)
+    c_exp = 1.4426950408889634 / 8.0
+
+    def norm(x, gain, xh_ref, r_ref, rows):
+        center = x - per_head(x, mean_m)
+        spread = per_head(center * center, mean_m)
+        r = lax.rsqrt(spread + EPS)
+        xh = center * r
+        xh_ref[rows, :] = xh
+        r_ref[rows, :] = r
+        return (xh * gain).astype(BF)
+
+    def project(i, carry):
+        rows = pl.ds(pl.multiple_of(i * RB, RB), RB)
+        y = dot_nn(nrm[rows, :], wqkv[...])
+        q = norm(y[:, :128], gq[...], xq, rq, rows)
+        k = norm(y[:, 128:256], gk[...], xk, rk, rows)
+        v = y[:, 256:]
+        qp[rows, :] = q
+        hi, lo = two_parts(q.astype(F32) * c_exp)
+        hi, lo = hi.astype(F32), lo.astype(F32)
+        qa[0, rows, :] = jnp.where(first, hi, pltpu.roll(lo, HD, 1)).astype(BF)
+        qa[1, rows, :] = jnp.where(first, pltpu.roll(hi, HD, 1), lo).astype(BF)
+        kf = k.astype(F32)
+        kr = pltpu.roll(kf, HD, 1)
+        kb[0, rows, :] = jnp.where(first, kf, kr).astype(BF)
+        kb[1, rows, :] = jnp.where(first, kr, kf).astype(BF)
+        vv[0, rows, :] = jnp.where(first, v, 1.0).astype(BF)
+        vv[1, rows, :] = jnp.where(first, 1.0, v).astype(BF)
+        do[rows, :] = dot_nt(cot[rows, :], wo[...]).astype(BF)
+        zero = jnp.zeros((RB, 128), F32)
+        dq[rows, :] = zero
+        dk[rows, :] = zero
+        dv[rows, :] = zero
+        att_o[rows, :] = zero.astype(BF)
+        return carry
+
+    lax.fori_loop(0, nb, project, 0)
+
+    def block(q_rows, k_rows, n_q, n_k, masked, add):
+        ps, pbs, xs = [], [], []
+        for h in range(2):
+            p = jnp.exp2(dot_nt(qa[h, q_rows, :], kb[h, k_rows, :]))
+            if masked:
+                keep = lax.broadcasted_iota(jnp.int32, (n_q, n_k), 1) < SMALL
+                p = jnp.where(keep, p, 0.0)
+            pb = p.astype(BF)
+            ps.append(p)
+            pbs.append(pb)
+            xs.append(dot_nn(pb, vv[h, k_rows, :]))
+        total = jnp.where(first, pltpu.roll(xs[0], HD, 1), pltpu.roll(xs[1], HD, 1))
+        inverse = 1.0 / total
+        out = jnp.where(first, xs[0], xs[1]) * inverse
+        att_o[q_rows, :] = out.astype(BF)
+        grad = do[q_rows, :].astype(F32)
+        inner = per_head(grad * out, sum_m) * inverse
+        scaled = (grad * inverse).astype(BF)
+        scaled_f = scaled.astype(F32)
+        i_hi, i_lo = two_parts(inner)
+        i_hi, i_lo = i_hi.astype(F32), i_lo.astype(F32)
+        dqs, dks, dvs = [], [], []
+        for h in range(2):
+            own = first if h == 0 else jnp.logical_not(first)
+            base = HD * (1 - h)
+            other = pltpu.roll(i_hi, HD, 1), pltpu.roll(i_lo, HD, 1)
+            side = jnp.where(lane == base, -other[0], jnp.where(lane == base + 1, -other[1], 0.0))
+            left = jnp.where(own, scaled_f, side).astype(BF)
+            ds = (ps[h] * dot_nt(left, vv[h, k_rows, :])).astype(BF)
+            dqs.append(dot_nn(ds, kb[h, k_rows, :]))
+            dks.append(dot_tn(ds, qp[q_rows, :]))
+            dvs.append(dot_tn(pbs[h], scaled))
+        dq[q_rows, :] = jnp.where(first, dqs[0], dqs[1])
+        new_k = jnp.where(first, dks[0], dks[1])
+        new_v = jnp.where(first, dvs[0], dvs[1])
+        if add:
+            dk[k_rows, :] += new_k
+            dv[k_rows, :] += new_v
+        else:
+            dk[k_rows, :] = new_k
+            dv[k_rows, :] = new_v
+
+    for s in range(2):
+        base, big, count = info[1 + 3 * s], info[2 + 3 * s], info[3 + 3 * s]
+
+        @pl.when(big == 1)
+        def _():
+            k_rows = pl.ds(pl.multiple_of(base, 16), BIG)
+
+            def one(i, carry):
+                block(pl.ds(pl.multiple_of(base + i * 256, 16), 256), k_rows, 256, BIG, False, True)
+                return carry
+
+            lax.fori_loop(0, BIG // 256, one, 0)
+
+        def small(i, carry):
+            rows = pl.ds(pl.multiple_of(base + big * BIG + i * BLK, 16), BLK)
+            block(rows, rows, BLK, BLK, True, False)
+            return carry
+
+        lax.fori_loop(0, count, small, 0)
+
+    dw[...] = jnp.zeros_like(dw)
+    dwo[...] = jnp.zeros_like(dwo)
+    dg[...] = jnp.zeros_like(dg)
+
+    def pull(g_out, gain, xh, r, slot):
+        dg[slot : slot + 1, :] += jnp.sum(g_out * xh, axis=0, keepdims=True)
+        g = g_out * gain
+        return r * (g - per_head(g, mean_m) - xh * per_head(g * xh, mean_m))
+
+    def finish(i, carry):
+        rows = pl.ds(pl.multiple_of(i * RB, RB), RB)
+        gq_pre = pull(dq[rows, :] * 0.125, gq[...], xq[rows, :], rq[rows, :], 0)
+        gk_pre = pull(dk[rows, :] * 0.125, gk[...], xk[rows, :], rk[rows, :], 1)
+        g = jnp.concatenate([gq_pre, gk_pre, dv[rows, :]], axis=1).astype(BF)
+        dqkv_o[rows, :] = g
+        dw[...] += dot_tn(g, nrm[rows, :])
+        dwo[...] += dot_tn(att_o[rows, :], cot[rows, :])
+        return carry
+
+    lax.fori_loop(0, nb, finish, 0)
+    dw_o[...] = dw[...].astype(BF)
+    dwo_o[...] = dwo[...].astype(BF)
+    dgq_o[...] = dg[0:1, :]
+    dgk_o[...] = dg[1:2, :]
+
+
+def attention(info, nrm, cot, wqkv, wo, gq, gk):
+    sds = jax.ShapeDtypeStruct
+    outs = (sds((ROWS, 128), BF), sds((ROWS, 384), BF), sds((384, D), BF), sds((128, D), BF),
+            sds((1, 128), F32), sds((1, 128), F32))
+    v = pltpu.VMEM
+    scratch = [v((2, ROWS, 128), BF)] * 3 + [v((ROWS, 128), BF)] * 2 + [v((ROWS, 128), F32)] * 7 + [
+        v((384, D), F32), v((128, D), F32), v((8, 128), F32)]
+    return call(attention_body, outs, scratch, (info, nrm, cot, wqkv, wo, gq, gk),
+                [SCALARS] + [ANYWHERE] * 6, cost=(12 * 10**9, 14 * 10**6))
+
+
+def mlp_body(info, nrm, cot, win, wout, bias, act_o, gm_o, dwin_o, dwout_o, db_o, dwin, dwout, db):
+    i = pl.program_id(0)
+
+    @pl.when(i == 0)
+    def _():
+        dwin[...] = jnp.zeros_like(dwin)
+        dwout[...] = jnp.zeros_like(dwout)
+        db[...] = jnp.zeros_like(db)
+
+    @pl.when(i < info[0])
+    def _():
+        x = nrm[...]
+        g = cot[...]
+        pre = dot_nn(x, win[...]) + bias[...]
+        ga = dot_nt(g, wout[...])
+        c0 = 0.7978845608028654
+        c1 = 0.044715 * c0
+        sq = pre * pre
+        t = jnp.tanh(pre * (c0 + c1 * sq))
+        half = 0.5 * pre
+        up = 1.0 + t
+        act = (half * up).astype(BF)
+        slope = 0.5 * up + half * (1.0 - t * t) * (c0 + 3.0 * c1 * sq)
+        gmf = ga * slope
+        gm = gmf.astype(BF)
+        act_o[...] = act
+        gm_o[...] = gm
+        db[...] += jnp.sum(gmf, axis=0, keepdims=True)
+        dwout[...] += dot_tn(act, g)
+        dwin[...] += dot_tn(gm, x)
+
+    @pl.when(i == pl.num_programs(0) - 1)
+    def _():
+        dwin_o[...] = dwin[...].astype(BF)
+        dwout_o[...] = dwout[...].astype(BF)
+        db_o[...] = db[...]
+
+
+def clamp(i, info):
+    return (jnp.minimum(i, info[0] - 1), 0)
+
+
+def whole(i, info):
+    return (0, 0)
+
+
+def mlp(info, nrm, cot, win, wout, bias):
+    sds = jax.ShapeDtypeStruct
+    outs = (sds((ROWS, U), BF), sds((ROWS, U), BF), sds((U, D), BF), sds((U, D), BF), sds((1, U), F32))
+    bs = pl.BlockSpec
+    in_specs = [bs((RB, D), clamp), bs((RB, D), clamp), bs((D, U), whole), bs((U, D), whole), bs((1, U), whole)]
+    out_specs = (bs((RB, U), clamp), bs((RB, U), clamp), bs((U, D), whole), bs((U, D), whole), bs((1, U), whole))
+    v = pltpu.VMEM
+    scratch = [v((U, D), F32), v((U, D), F32), v((1, U), F32)]
+    return call(mlp_body, outs, scratch, (info, nrm, cot, win, wout, bias), in_specs, out_specs,
+                grid=(NRB,), prefetch=1, cost=(10 * 10**9, 18 * 10**6))
+
+
+def sums_body(info, *refs, n, transposed):
+    i = pl.program_id(0)
+    lefts, rights, out = refs[:n], refs[n : 2 * n], refs[2 * n]
+
+    @pl.when(i < info[0])
+    def _():
+        total = None
+        for a, b, t in zip(lefts, rights, transposed):
+            part = dot_nt(a[...], b[...]) if t else dot_nn(a[...], b[...])
+            total = part if total is None else total + part
+        out[...] = total.astype(BF)
+
+    @pl.when(i >= info[0])
+    def _():
+        out[...] = jnp.zeros_like(out)
+
+
+def sums(info, lefts, rights, transposed):
+    n = len(lefts)
+    bs = pl.BlockSpec
+    in_specs = [bs((RB, a.shape[1]), clamp) for a in lefts] + [bs(b.shape, whole) for b in rights]
+    k = sum(a.shape[1] for a in lefts)
+    return call(functools.partial(sums_body, n=n, transposed=transposed), jax.ShapeDtypeStruct((ROWS, D), BF), [],
+                (info, *lefts, *rights), in_specs, bs((RB, D), lambda i, info: (i, 0)), grid=(NRB,), prefetch=1,
+                cost=(2 * 2304 * k * D, 2 * 2304 * (k + D)))
+
+
+def prepare_body(src, tokens, cot, gain, x_o, nrm_o, cot_o, gob_o):
+    i = pl.program_id(0)
+    pick = (src[...] == lax.broadcasted_iota(jnp.int32, (BLK, tokens.shape[0]), 1)).astype(BF)
+    x = dot_nn(pick, tokens[...])
+    g = dot_nn(pick, cot[...])
+    x_o[...] = x.astype(BF)
+    cot_o[...] = g.astype(BF)
+    center = x - jnp.mean(x, axis=1, keepdims=True)
+    spread = jnp.mean(center * center, axis=1, keepdims=True)
+    nrm_o[...] = (center * lax.rsqrt(spread + EPS) * gain[...]).astype(BF)
+
+    @pl.when(i == 0)
+    def _():
+        gob_o[...] = jnp.zeros_like(gob_o)
+
+    gob_o[...] += jnp.sum(g, axis=0, keepdims=True)
+
+
+def prepare(src, tokens, cot, gain):
+    sds = jax.ShapeDtypeStruct
+    bs = pl.BlockSpec
+    cap = tokens.shape[0]
+    row = bs((BLK, D), lambda i: (i, 0))
+    fixed = lambda i: (0, 0)
+    return call(prepare_body, (sds((CAN, D), BF),) * 3 + (sds((1, D), F32),), [], (src, tokens, cot, gain),
+                [bs((BLK, 1), lambda i: (i, 0)), bs((cap, D), fixed), bs((cap, D), fixed), bs((1, D), fixed)],
+                (row, row, row, bs((1, D), fixed)), grid=(CAN // BLK,), cost=(6 * 10**9, 13 * 10**6))
+
+
+def back_rows(dst, held, out):
+    cap = out.shape[0]
+    for at in range(0, cap, 480):
+        n = min(480, cap - at)
+        pick = (dst[at : at + n, :] == lax.broadcasted_iota(jnp.int32, (n, CAN), 1)).astype(BF)
+        out[at : at + n, :] = dot_nn(pick, held[...]).astype(BF)
+
+
+def output_body(dst, x, a, b, bias, out, held):
+    for i in range(CAN // BLK):
+        rows = pl.ds(i * BLK, BLK)
+        held[rows, :] = (x[rows, :].astype(F32) + (a[rows, :].astype(F32) + b[rows, :].astype(F32) + bias[...])).astype(BF)
+    back_rows(dst, held, out)
+
+
+def gradient_body(dst, x, a, b, cot, gain, out, held):
+    for i in range(CAN // BLK):
+        rows = pl.ds(i * BLK, BLK)
+        v = x[rows, :].astype(F32)
+        center = v - jnp.mean(v, axis=1, keepdims=True)
+        r = lax.rsqrt(jnp.mean(center * center, axis=1, keepdims=True) + EPS)
+        xh = center * r
+        g = (a[rows, :].astype(F32) + b[rows, :].astype(F32)) * gain[...]
+        gx = r * (g - jnp.mean(g, axis=1, keepdims=True) - xh * jnp.mean(g * xh, axis=1, keepdims=True))
+        held[rows, :] = (cot[rows, :].astype(F32) + gx).astype(BF)
+    back_rows(dst, held, out)
+
+
+def last_rows(body, cap, args):
+    return call(body, jax.ShapeDtypeStruct((cap, D), BF), [pltpu.VMEM((CAN, D), BF)], args, [ANYWHERE] * len(args),
+                cost=(4 * 10**9, 12 * 10**6))
+
+
+def unit_ranges(c, j):
+    first = [(96 * c + 32 * j, 32)]
+    return first + [(192 + 480 * s + 240 * c + 80 * j, 80) for s in range(6)]
+
+
+def split_body(place, w_in, w_out, *outs):
+    c, f = place[0], place[1]
+    for cc in range(2):
+
+        @pl.when(c == cc)
+        def _():
+            for p in range(3):
+                for n in range(3):
+                    at = D * n + 384 * cc + 128 * p
+                    outs[p][96 * n : 96 * n + 96, :] = w_in[:, at : at + 128]
+            for j in range(3):
+                cols = [w_in[:, 3 * D + u : 3 * D + u + n] for u, n in unit_ranges(cc, j)]
+                m = jnp.concatenate(cols, axis=1)
+                outs[3 + j][0:96, :] = m[:, :256]
+                outs[3 + j][96:192, :] = m[:, 256:]
+            outs[6][...] = w_out[:, 384 * cc : 384 * cc + 384]
+            for j in range(3):
+                for t in range(3):
+                    lanes = slice(256 * t, 256 * t + 256)
+                    at = 192 + 80 * t
+
+                    @pl.when(f != 1)
+                    def _():
+                        outs[3 + j][at : at + 80, :] = w_out[240 * cc + 80 * j : 240 * cc + 80 * j + 80, lanes]
+
+                    @pl.when(f == 1)
+                    def _():
+                        a, b = 144 * cc + 48 * j, 288 + 96 * cc + 32 * j
+                        outs[3 + j][at : at + 48, :] = w_out[a : a + 48, lanes]
+                        outs[3 + j][at + 48 : at + 80, :] = w_out[b : b + 32, lanes]
+
+
+def split(place, w_in, w_out):
+    sds = jax.ShapeDtypeStruct
+    outs = (sds((288, 128), BF),) * 3 + (sds((432, 256), BF),) * 3 + (sds((480, 384), BF),)
+    return call(split_body, outs, [], (place, w_in, w_out), [SCALARS, ANYWHERE, ANYWHERE], cost=(0, 4 * 10**6))
+
+
+def slot_of(place, f):
+    dz = place[3] ^ (f >> 1)
+    return place[2] ^ (f & 1), ((dz & 1) << 1) | (dz >> 1)
+
+
+def taken(place, near, far, f):
+    side, at = slot_of(place, f)
+    return jnp.where(side == 0, near[at], far[at])
+
+
+def join_pair_body(place, near, far, w):
+    for f in range(8):
+        piece = taken(place, near, far, f)
+        for n in range(3):
+            w[96 * f : 96 * f + 96, 128 * n : 128 * n + 128] = piece[96 * n : 96 * n + 96]
+
+
+def join_pair(place, near, far):
+    return call(join_pair_body, jax.ShapeDtypeStruct((D, 384), BF), [], (place, near, far), [SCALARS, ANYWHERE, ANYWHERE],
+                cost=(0, 2 * 10**6))
+
+
+def join_chunk_body(place, near, far, win, wout):
+    for f in range(8):
+        piece = taken(place, near, far, f)
+        for n in range(2):
+            win[96 * f : 96 * f + 96, 256 * n : 256 * n + 256] = piece[96 * n : 96 * n + 96]
+        for t in range(3):
+            part = piece[192 + 80 * t : 272 + 80 * t]
+            lanes = slice(256 * t, 256 * t + 256)
+            if f == 1:
+                wout[0:32, lanes] = part[48:]
+            elif f > 1:
+                wout[80 * f - 128 : 80 * f - 48, lanes] = part
+
+
+def join_chunk(place, near, far):
+    sds = jax.ShapeDtypeStruct
+    return call(join_chunk_body, (sds((D, U), BF), sds((U, D), BF)), [], (place, near, far), [SCALARS, ANYWHERE, ANYWHERE],
+                cost=(0, 4 * 10**6))
+
+
+def put(place, near, far, f, fill):
+    side, at = slot_of(place, f)
+
+    @pl.when(side == 0)
+    def _():
+        fill(near.at[at])
+
+    @pl.when(side != 0)
+    def _():
+        fill(far.at[at])
+
+
+def cut_pair_body(place, dw, near, far):
+    full = jnp.transpose(dw[...].astype(F32)).astype(BF)
+    for f in range(8):
+
+        def fill(ref, f=f):
+            for n in range(3):
+                ref[96 * n : 96 * n + 96, :] = full[96 * f : 96 * f + 96, 128 * n : 128 * n + 128]
+
+        put(place, near, far, f, fill)
+
+
+def cut_pair(place, dw):
+    sds = jax.ShapeDtypeStruct
+    return call(cut_pair_body, (sds((4, 288, 128), BF),) * 2, [], (place, dw), [SCALARS, ANYWHERE], cost=(0, 2 * 10**6))
+
+
+def cut_chunk_body(place, dwin, dwout, slots, near, far):
+    full = jnp.transpose(dwin[...].astype(F32)).astype(BF)
+    for f in range(8):
+
+        def fill(ref, f=f):
+            for n in range(2):
+                ref[96 * n : 96 * n + 96, :] = full[96 * f : 96 * f + 96, 256 * n : 256 * n + 256]
+            for t in range(3):
+                lanes = slice(256 * t, 256 * t + 256)
+                at = 192 + 80 * t
+                if f == 0:
+                    ref[at : at + 80, :] = slots[0:80, lanes]
+                elif f == 1:
+                    ref[at : at + 48, :] = slots[80:128, lanes]
+                    ref[at + 48 : at + 80, :] = dwout[0:32, lanes]
+                else:
+                    ref[at : at + 80, :] = dwout[80 * f - 128 : 80 * f - 48, lanes]
+
+        put(place, near, far, f, fill)
+
+
+def cut_chunk(place, dwin, dwout, slots):
+    sds = jax.ShapeDtypeStruct
+    return call(cut_chunk_body, (sds((4, 432, 256), BF),) * 2, [], (place, dwin, dwout, slots),
+                [SCALARS] + [ANYWHERE] * 3, cost=(0, 4 * 10**6))
+
+
+def final_body(place, w_in, ln, *refs):
+    own, other = refs[:6], refs[6:12]
+    gin, gout, gln = refs[12:]
+    c, f = place[0], place[1]
+    for cc in range(2):
+        sources = [jnp.where(c == cc, a[...], b[...]) for a, b in zip(own, other)]
+        for p in range(3):
+            for n in range(3):
+                at = D * n + 384 * cc + 128 * p
+                gin[:, at : at + 128] = sources[p][96 * n : 96 * n + 96, :]
+        for j in range(3):
+            s = sources[3 + j]
+            m = jnp.concatenate([s[0:96], s[96:192]], axis=1)
+            done = 0
+            for u, n in unit_ranges(cc, j):
+                gin[:, 3 * D + u : 3 * D + u + n] = m[:, done : done + n]
+                done += n
+            for t in range(3):
+                lanes = slice(256 * t, 256 * t + 256)
+                part = s[192 + 80 * t : 272 + 80 * t]
+
+                @pl.when(f != 1)
+                def _():
+                    gout[240 * cc + 80 * j : 240 * cc + 80 * j + 80, lanes] = part
+
+                @pl.when(f == 1)
+                def _():
+                    a, b = 144 * cc + 48 * j, 288 + 96 * cc + 32 * j
+                    gout[a : a + 48, lanes] = part[:48]
+                    gout[b : b + 32, lanes] = part[48:]
+    total = jnp.sum(w_in[...].astype(F32) * gin[...], axis=1, keepdims=True)
+    gln[...] = total / ln[...]
+
+
+def final(place, w_in, ln, own, other):
+    sds = jax.ShapeDtypeStruct
+    outs = (sds((96, 7 * D), F32), sds((480, D), F32), sds((96, 1), F32))
+    return call(final_body, outs, [], (place, w_in, ln, *own, *other), [SCALARS] + [ANYWHERE] * 14, cost=(0, 10**7))
+
+
+def routes():
+    places = [(x, c, z, y) for x in range(2) for c in range(2) for z in range(4) for y in range(2)]
+    number = lambda x, c, z, y: (x * 2 + c) * 8 + z * 2 + y
+    pairs = lambda move: [(number(*p), number(*move(*p))) for p in places]
+    out = {
+        "core": pairs(lambda x, c, z, y: (x, 1 - c, z, y)),
+        "x": pairs(lambda x, c, z, y: (1 - x, c, z, y)),
+        "y": pairs(lambda x, c, z, y: (x, c, z, 1 - y)),
+        "z1": pairs(lambda x, c, z, y: (x, c, z ^ 1, y)),
+        "z2": pairs(lambda x, c, z, y: (x, c, z ^ 2, y)),
+    }
+    at = lambda n: (n % 8) // 2
+    out["z2_up"] = [(a, b) for a, b in out["z2"] if at(a) == 0]
+    out["z1_up"] = [(a, b) for a, b in out["z1"] if at(a) % 2 == 0]
+    return out
+
+
+def images(lengths, assign, device):
+    own = assign == device
+    small = own & (lengths == SMALL)
+    large = own & (lengths == BIG)
+    number = lax.iota(jnp.int32, lengths.shape[0])
+    count = jnp.sum(small.astype(jnp.int32))
+    has = jnp.sum(large.astype(jnp.int32))
+    at = jnp.sum(jnp.where(large, number, 0))
+    before = jnp.where(has > 0, jnp.sum((small & (number < at)).astype(jnp.int32)), count)
+    return count, has, before
+
+
+def row_tables(count, has, before, cap):
+    row = lax.broadcasted_iota(jnp.int32, (CAN, 1), 0)
+    rest = row - BIG * has
+    slot, offset = rest // BLK, rest % BLK
+    small_src = slot * SMALL + offset + jnp.where(slot >= before, BIG * has, 0)
+    src = jnp.where(rest < 0, SMALL * before + row, jnp.where((offset < SMALL) & (slot < count), small_src, -1))
+    row = lax.broadcasted_iota(jnp.int32, (cap, 1), 0)
+    rest = row - SMALL * before
+    inside = (rest >= 0) & (rest < BIG * has)
+    rest = row - jnp.where(rest >= BIG * has, BIG * has, 0)
+    slot, offset = rest // SMALL, rest % SMALL
+    dst = jnp.where(inside, row - SMALL * before, jnp.where(slot < count, BIG * has + slot * BLK + offset, -1))
+    return src, dst
+
+
+def per_device_paired(
+    tokens, lengths, assign, w_in, w_out, ln_scale, q_scale, k_scale, mlp_bias, out_bias, cotangent
+):
+    way = routes()
+    go = lambda v, name: lax.ppermute(v, ("rep", "fsdp"), way[name])
+    rep, f = lax.axis_index("rep"), lax.axis_index("fsdp")
+    c, y, z = rep % 2, f % 2, f // 2
+    cap = tokens.shape[0]
+    place = jnp.stack([c, f, y, z]).astype(jnp.int32)
+
+    device = rep * 8 + f
+    count, has, before = images(lengths, assign, device)
+    count_b, has_b, _ = images(lengths, assign, device + 8 - 16 * c)
+    src, dst = row_tables(count, has, before, cap)
+    blocks, blocks_b = jnp.where(has > 0, 7, count), jnp.where(has_b > 0, 7, count_b)
+    base = BLK * blocks
+    active = (BLK * (blocks + blocks_b) + RB - 1) // RB
+    info = jnp.stack([active, 0 * base, has, count, base, has_b, count_b, 0 * base]).astype(jnp.int32)
+
+    def gather(piece):
+        two = jnp.stack([piece, go(piece, "z2")])
+        four = jnp.concatenate([two, go(two, "z1")])
+        return four, go(four, "y")
+
+    packed = jnp.concatenate([ln_scale, q_scale, k_scale, mlp_bias, out_bias, jnp.zeros((48,), BF)]).reshape(5, 128)
+    small = jnp.concatenate(gather(packed)).reshape(8, 640)
+    shard = lax.iota(jnp.int32, 8)
+    dz = z ^ (shard >> 1)
+    position = 4 * (y ^ (shard & 1)) + (((dz & 1) << 1) | (dz >> 1))
+    order = (position[:, None] == shard[None, :]).astype(BF)
+    small = dot_nn(order, small)
+    ln = small[:, :96].reshape(1, D)
+    gq = jnp.tile(small[:, 96:104].reshape(1, HD), (1, 2))
+    gk = jnp.tile(small[:, 104:112].reshape(1, HD), (1, 2))
+    mb = small[:, 112:496].reshape(4 * D)
+    ob = small[:, 496:592].reshape(1, D)
+    mb = jnp.concatenate([mb[:192].reshape(2, 3, 32), mb[192:].reshape(6, 2, 3, 80).transpose(1, 2, 0, 3).reshape(2, 3, 480)], axis=2)
+    mb = lax.dynamic_index_in_dim(mb, c, 0, False)
+
+    pieces = split(place, w_in, w_out)
+    wqkv = [join_pair(place, *gather(piece)) for piece in pieces[:3]]
+    wo = pieces[6]
+    wo = jnp.where(z == 0, wo, go(wo, "z2_up"))
+    wo = jnp.where(z % 2 == 0, wo, go(wo, "z1_up"))
+    wo_b = go(wo, "y")
+    wo = jnp.concatenate([jnp.where(y == 0, wo, wo_b), jnp.where(y == 0, wo_b, wo)[:288]])
+    mine = lax.dynamic_slice_in_dim(wo, 384 * c, 384, 0)
+    theirs = go(lax.dynamic_slice_in_dim(wo, 384 - 384 * c, 384, 0), "core")
+    wo = jnp.where(c == 0, jnp.concatenate([mine, theirs], axis=1), jnp.concatenate([theirs, mine], axis=1))
+    chunks = [join_chunk(place, *gather(piece)) for piece in pieces[3:6]]
+
+    x, nrm, cot, gob = prepare(src, tokens, cotangent, ln)
+
+    def both(own):
+        full = jnp.pad(own, ((0, ROWS - CAN), (0, 0)))
+        return lax.dynamic_update_slice(full, go(own, "core"), (base, jnp.int32(0)))
+
+    nrm2, cot2 = both(nrm), both(cot)
+
+    def scatter(near, far):
+        add = lambda a, b: (a.astype(F32) + b.astype(F32)).astype(BF)
+        four = go(far, "y")
+        s_near, s_far = add(near[:2], four[:2]), add(near[2:], four[2:])
+        two = go(s_far, "z1")
+        one = add(s_near[0], two[0])
+        one = add(one, go(add(s_near[1], two[1]), "z2"))
+        total = one.astype(F32) + go(one, "x").astype(F32)
+        return total, go(total, "core")
+
+    att, dqkv, dwo, dgq, dgk, reduced = [], [], [], 0.0, 0.0, []
+    for p in range(3):
+        a, dj, dw, dwo_p, dgq_p, dgk_p = attention(info, nrm2, cot2, wqkv[p], wo[128 * p : 128 * p + 128], gq, gk)
+        att.append(a)
+        dqkv.append(dj)
+        dwo.append(dwo_p)
+        dgq, dgk = dgq + dgq_p, dgk + dgk_p
+        reduced.append(scatter(*cut_pair(place, dw)))
+    dwo = jnp.concatenate(dwo)
+    recv = go(lax.dynamic_slice_in_dim(dwo, 240 - 144 * c, 144, 0), "core")
+    slots = jnp.where(c == 0, jnp.concatenate([dwo[:240], recv]), jnp.concatenate([recv, dwo[:96], dwo[240:]]))
+
+    act, gm, dbs = [], [], []
+    for j in range(3):
+        a, g, dwin, dwout, db = mlp(info, nrm2, cot2, *chunks[j], mb[j : j + 1])
+        act.append(a)
+        gm.append(g)
+        dbs.append(db)
+        slot = jnp.concatenate([slots[80 * j : 80 * j + 80], slots[240 + 48 * j : 288 + 48 * j]])
+        reduced.append(scatter(*cut_chunk(place, dwin, dwout, slot)))
+
+    db = jnp.concatenate(dbs, axis=0).reshape(12, 128)
+    none = jnp.zeros_like(db)
+    vec = jnp.concatenate([gob.reshape(6, 128), dgq, dgk, jnp.where(c == 0, db, none), jnp.where(c == 0, none, db)])
+    for name in ("core", "x", "y", "z1", "z2"):
+        vec = vec + go(vec, name)
+    g_ob = lax.dynamic_slice_in_dim(vec[:6].reshape(D), 96 * f, 96, 0)
+    g_qs = lax.dynamic_slice_in_dim(vec[6, :HD] + vec[6, HD:], 8 * f, 8, 0)
+    g_ks = lax.dynamic_slice_in_dim(vec[7, :HD] + vec[7, HD:], 8 * f, 8, 0)
+    g_mb = vec[8:].reshape(2, 3, U)
+    g_mb = jnp.concatenate([g_mb[:, :, :32].reshape(192), g_mb[:, :, 32:].reshape(2, 3, 6, 80).transpose(2, 0, 1, 3).reshape(2880)])
+    g_mb = lax.dynamic_slice_in_dim(g_mb, 384 * f, 384, 0)
+
+    def exchanged(part):
+        return part[:CAN], go(lax.dynamic_slice_in_dim(part, base, CAN, 0), "core")
+
+    part = sums(info, att + act, [wo[128 * p : 128 * p + 128] for p in range(3)] + [w for _, w in chunks], [False] * 6)
+    output = last_rows(output_body, cap, (dst, x, *exchanged(part), ob))
+    part = sums(info, dqkv + gm, wqkv + [w for w, _ in chunks], [True] * 6)
+    grad_tokens = last_rows(gradient_body, cap, (dst, x, *exchanged(part), cot, ln))
+
+    own_ln = ln_scale.astype(F32).reshape(96, 1)
+    g_win, g_wout, g_ln = final(place, w_in, own_ln, [r[0] for r in reduced], [r[1] for r in reduced])
+    return output, grad_tokens, g_win, g_wout, g_ln.reshape(96), g_qs, g_ks, g_mb, g_ob
+
+
 HEADS = 12
-HD = 64
-
-
 epsilon = 1e-06
 
 
@@ -211,6 +904,7 @@
         P("fsdp"),
         P("fsdp"),
     )
+    paired = dict(mesh.shape) == {"rep": 4, "fsdp": 8}
     return jax.shard_map(
-        per_device, mesh=mesh, in_specs=in_specs, out_specs=out_specs, check_vma=False
-    )
+        per_device_paired if paired else per_device, mesh=mesh, in_specs=in_specs, out_specs=out_specs, check_vma=False
+    )

time: 1310 us -> 593 us (0.45)
  matrix products: 445 us -> 0.19 us
  waiting for transfers between devices: 404 us -> 179 us
  Pallas kernels: 0 us -> 196 us
  other arithmetic: 197 us -> 23.3 us
  starting transfers between devices: 0.2 us -> 150 us
  blocking collectives: 93.5 us -> 0 us
  local copies, waits for them, and re-layouts: 108 us -> 42 us
  loops' own time: 39 us -> 0 us
    dot_general x90 -> x1, matrix products: 445 us -> 0.19 us  [dot_nn(): lax.dot_general(a, b, (((1,), (0,)), ((), ())), preferred_element_type=F32)]
    reduce_scatter x2 -> x0, waiting for transfers between devices: 203 us -> none  [the longest x1 203 us: per_device(): lax.psum_scatter(grads[0], 'fsdp', scatter_dimension=0, tiled=True)]
    pallas_call x0 -> x25, Pallas kernels: none -> 196 us  [call(): pl.pallas_call(body, grid_spec=spec, out_shape=out_shape, compiler_params...]
    ppermute x0 -> x65, waiting for transfers between devices: none -> 179 us  [per_device_paired(): go = lambda v, name: lax.ppermute(v, ('rep', 'fsdp'), way[name])]
    ppermute x0 -> x65, starting transfers between devices: none -> 150 us  [per_device_paired(): go = lambda v, name: lax.ppermute(v, ('rep', 'fsdp'), way[name])]
    all_gather x2 -> x0, waiting for transfers between devices: 137 us -> none  [the longest x1 103 us: per_device(): lax.all_gather(params[0], 'fsdp', axis=0, tiled=True)]
    convert_element_type x18, other arithmetic: 112 us -> 4.59 us  [scatter(): add = lambda a, b: (a.astype(F32) + b.astype(F32)).astype(BF)]
    reduce_sum x25 -> x2, other arithmetic: 74.2 us -> 3.34 us  [the longest x1 2.02 us: images(): count = jnp.sum(small.astype(jnp.int32))]
  transfers between devices with their start and end apart: 5 -> 65, of which waited for: 4 -> 27; matrix products, arithmetic and copies ran while one was open for 39% -> 9% of each run, Pallas kernels for 0% -> 28%
where the time goes in v1:
time: 593 us; the launch traced here: 597 us
  Pallas kernels  196 us (33%)
  waiting for transfers between devices  179 us (30%)
  starting transfers between devices  150 us (25%)
  local copies, waits for them, and re-layouts  42 us (7%)
  other arithmetic  23.3 us (4%)
  between operations  6.67 us (1%)
    pallas_call x25, Pallas kernels, call(): pl.pallas_call(body, grid_spec=spec, out_shape=out_shape, compiler_params...  196 us
    ppermute x65, waiting for transfers between devices, per_device_paired(): go = lambda v, name: lax.ppermute(v, ('rep', 'fsdp'), way[name])  179 us
    ppermute x65, starting transfers between devices, per_device_paired(): go = lambda v, name: lax.ppermute(v, ('rep', 'fsdp'), way[name])  150 us
  transfers between devices with their start and end apart: 65, of which 27 were waited for; matrix products, arithmetic and copies ran while one was open for 9% of the time, Pallas kernels for 28%

profile of v1, /device:TPU:0, one launch (start us, length us, event | category | flops | bytes accessed | tf_op | source)
XLA Modules:
  0.0 596.8 jit_solution(4414047894176767817)
XLA Ops:
  0.7 3.5 concatenate.89
  4.2 4.0 collective-permute-start
  8.8 2.8 shard_map.179
  11.6 2.9 collective-permute-start.12
  14.5 2.9 collective-permute-start.18
  23.4 2.6 fusion.12.dst
  25.9 2.5 select_select_fusion.src
  30.1 2.4 collective-permute-done.1
  36.8 3.1 stack.104.info
  43.4 12.4 %shard_map.178 = (bf16[1456,768]{1,0:T(8,128)(2,1)}, bf16[1456,768]{1,0:T(8,128)(2,1)}, bf16[1456,768]{1,0:T(8,128)(2,1)}, f32[1,768]{1,0:T(1,128)}) custom-call(s32[1456,1]{1,0:T(8,128)} %select_select_fusion.src, bf16[1416,768]{1,0:T(8,128)(2,1)} %tokens.1, bf16[1416,768]{1,0:T(8,128)(2,1)} %cot.1, f32[1,768]{1,0:T(1,128)} %reshape.393.gain), custom_call_target="tpu_custom_call" | custom-call | flops 6000000000 | bytes 13000000 | tf_op jit(solution)/shard_map/pallas_call | solution.py:57
  56.6 4.1 pad.7
  60.7 4.1 pad.8
  65.7 3.4 collective-permute-start.9
  69.2 3.0 collective-permute-start.24
  73.9 9.8 %collective-permute-done.24 = bf16[432,256]{1,0:T(8,128)(2,1)S(1)} collective-permute-done((bf16[432,256]{1,0:T(8,128)(2,1)S(1)}, bf16[432,256]{1,0:T(8,128)(2,1)S(1)}, u32[]{:S(2)}, u32[]{:S(2)}) %collective-permute-start.24) | collective-permute-done | bytes 221216 | tf_op jit(solution)/shard_map/ppermute | solution.py:591
  85.9 5.0 collective-permute-done.16
  93.8 11.4 %collective-permute-done.17.far = bf16[4,288,128]{2,1,0:T(8,128)(2,1)S(1)} collective-permute-done((bf16[4,288,128]{2,1,0:T(8,128)(2,1)S(1)}, bf16[4,288,128]{2,1,0:T(8,128)(2,1)S(1)}, u32[]{:S(2)}, u32[]{:S(2)}) %collective-permute-start.17) | collective-permute-done | bytes 294944 | tf_op jit(solution)/shard_map/ppermute | solution.py:591
  109.6 8.7 %collective-permute-done.22 = bf16[2,432,256]{2,1,0:T(8,128)(2,1)S(1)} collective-permute-done((bf16[2,432,256]{2,1,0:T(8,128)(2,1)S(1)}, bf16[2,432,256]{2,1,0:T(8,128)(2,1)S(1)}, u32[]{:S(2)}, u32[]{:S(2)}) %collective-permute-start.22) | collective-permute-done | bytes 442400 | tf_op jit(solution)/shard_map/ppermute | solution.py:591
  118.8 6.1 %collective-permute-done.25 = bf16[2,432,256]{2,1,0:T(8,128)(2,1)S(1)} collective-permute-done((bf16[2,432,256]{2,1,0:T(8,128)(2,1)S(1)}, bf16[2,432,256]{2,1,0:T(8,128)(2,1)S(1)}, u32[]{:S(2)}, u32[]{:S(2)}) %collective-permute-start.25) | collective-permute-done | bytes 442400 | tf_op jit(solution)/shard_map/ppermute | solution.py:591
  140.5 7.4 %collective-permute-done.26.far = bf16[4,432,256]{2,1,0:T(8,128)(2,1)} collective-permute-done((bf16[4,432,256]{2,1,0:T(8,128)(2,1)S(1)}, bf16[4,432,256]{2,1,0:T(8,128)(2,1)}, u32[]{:S(2)}, u32[]{:S(2)}) %collective-permute-start.26) | collective-permute-done | bytes 884768 | tf_op jit(solution)/shard_map/ppermute | solution.py:591
  147.9 2.8 shard_map.190
  150.7 16.2 %collective-permute-done.23.far = bf16[4,432,256]{2,1,0:T(8,128)(2,1)} collective-permute-done((bf16[4,432,256]{2,1,0:T(8,128)(2,1)S(1)}, bf16[4,432,256]{2,1,0:T(8,128)(2,1)}, u32[]{:S(2)}, u32[]{:S(2)}) %collective-permute-start.23) | collective-permute-done | bytes 884768 | tf_op jit(solution)/shard_map/ppermute | solution.py:591
  166.9 2.7 shard_map.188
  169.6 15.9 %collective-permute-done.20.far = bf16[4,432,256]{2,1,0:T(8,128)(2,1)} collective-permute-done((bf16[4,432,256]{2,1,0:T(8,128)(2,1)S(1)}, bf16[4,432,256]{2,1,0:T(8,128)(2,1)}, u32[]{:S(2)}, u32[]{:S(2)}) %collective-permute-start.20) | collective-permute-done | bytes 884768 | tf_op jit(solution)/shard_map/ppermute | solution.py:591
  185.4 2.8 shard_map.186
  188.2 3.2 constant_dynamic-update-slice_fusion.1.nrm
  191.4 3.2 constant_dynamic-update-slice_fusion.cot
  194.6 21.3 %shard_map.185 = (bf16[3072,128]{1,0:T(8,128)(2,1)}, bf16[3072,384]{1,0:T(8,128)(2,1)}, bf16[384,768]{1,0:T(8,128)(2,1)}, bf16[128,768]{1,0:T(8,128)(2,1)}, f32[1,128]{1,0:T(1,128)}, /*index=5*/f32[1,128]{1,0:T(1,128)}) custom-call(s32[8]{0:T(128)} %stack.104.info, bf16[3072,768]{1,0:T(8,128)(2,1)} %constant_dynamic-update-slice_fusion.1.nrm, ...), custom_call_target="tpu_custom_call" | custom-call | flops 12000000000 | bytes 14000000 | tf_op jit(solution)/shard_map/pallas_call | solution.py:57
  220.1 21.6 %shard_map.183 = (bf16[3072,128]{1,0:T(8,128)(2,1)}, bf16[3072,384]{1,0:T(8,128)(2,1)}, bf16[384,768]{1,0:T(8,128)(2,1)}, bf16[128,768]{1,0:T(8,128)(2,1)}, f32[1,128]{1,0:T(1,128)}, /*index=5*/f32[1,128]{1,0:T(1,128)}) custom-call(s32[8]{0:T(128)} %stack.104.info, bf16[3072,768]{1,0:T(8,128)(2,1)} %constant_dynamic-update-slice_fusion.1.nrm, ...), custom_call_target="tpu_custom_call" | custom-call | flops 12000000000 | bytes 14000000 | tf_op jit(solution)/shard_map/pallas_call | solution.py:57
  241.7 2.3 shard_map.197
  245.6 11.3 %shard_map.191 = (bf16[3072,512]{1,0:T(8,128)(2,1)}, bf16[3072,512]{1,0:T(8,128)(2,1)}, bf16[512,768]{1,0:T(8,128)(2,1)}, bf16[512,768]{1,0:T(8,128)(2,1)}, f32[1,512]{1,0:T(1,128)}) custom-call(s32[8]{0:T(128)} %stack.104.info, bf16[3072,768]{1,0:T(8,128)(2,1)} %constant_dynamic-update-slice_fusion.1.nrm, ...), custom_call_target="tpu_custom_call" | custom-call | flops 10000000000 | bytes 18000000 | tf_op jit(solution)/shard_map/pallas_call | solution.py:57
  256.9 11.3 %shard_map.189 = (bf16[3072,512]{1,0:T(8,128)(2,1)}, bf16[3072,512]{1,0:T(8,128)(2,1)}, bf16[512,768]{1,0:T(8,128)(2,1)}, bf16[512,768]{1,0:T(8,128)(2,1)}, f32[1,512]{1,0:T(1,128)}) custom-call(s32[8]{0:T(128)} %stack.104.info, bf16[3072,768]{1,0:T(8,128)(2,1)} %constant_dynamic-update-slice_fusion.1.nrm, ...), custom_call_target="tpu_custom_call" | custom-call | flops 10000000000 | bytes 18000000 | tf_op jit(solution)/shard_map/pallas_call | solution.py:57
  268.1 11.3 %shard_map.187 = (bf16[3072,512]{1,0:T(8,128)(2,1)}, bf16[3072,512]{1,0:T(8,128)(2,1)}, bf16[512,768]{1,0:T(8,128)(2,1)}, bf16[512,768]{1,0:T(8,128)(2,1)}, f32[1,512]{1,0:T(1,128)}) custom-call(s32[8]{0:T(128)} %stack.104.info, bf16[3072,768]{1,0:T(8,128)(2,1)} %constant_dynamic-update-slice_fusion.1.nrm, ...), custom_call_target="tpu_custom_call" | custom-call | flops 10000000000 | bytes 18000000 | tf_op jit(solution)/shard_map/pallas_call | solution.py:57
  280.3 21.3 %shard_map.181 = (bf16[3072,128]{1,0:T(8,128)(2,1)}, bf16[3072,384]{1,0:T(8,128)(2,1)}, bf16[384,768]{1,0:T(8,128)(2,1)}, bf16[128,768]{1,0:T(8,128)(2,1)}, f32[1,128]{1,0:T(1,128)}, /*index=5*/f32[1,128]{1,0:T(1,128)}) custom-call(s32[8]{0:T(128)} %stack.104.info, bf16[3072,768]{1,0:T(8,128)(2,1)} %constant_dynamic-update-slice_fusion.1.nrm, ...), custom_call_target="tpu_custom_call" | custom-call | flops 12000000000 | bytes 14000000 | tf_op jit(solution)/shard_map/pallas_call | solution.py:57
  308.2 74.1 %collective-permute-start.61 = (f32[32,128]{1,0:T(8,128)S(1)}, f32[32,128]{1,0:T(8,128)S(1)}, u32[]{:S(2)}, u32[]{:S(2)}) collective-permute-start(f32[32,128]{1,0:T(8,128)S(1)} %add.387), channel_id=1, source_target_pairs={{0,16},{1,17},{2,18},{3,19},{4,20},{5,21},{6,22},{7,23},{8,24},{9,... | collective-permute-start | bytes 49160 | tf_op jit(solution)/shard_map/ppermute | solution.py:591
  382.3 14.1 %shard_map.194 = bf16[3072,768]{1,0:T(8,128)(2,1)} custom-call(s32[8]{0:T(128)} %stack.104.info, bf16[3072,384]{1,0:T(8,128)(2,1)} %get-tuple-element.96.refs_0_, bf16[3072,384]{1,0:T(8,128)(2,1)} %get-tuple-element.97.refs_1_, bf16[3072,384]{1,0:T(8,128)(2,1)} %get-tuple-element.98.refs_2_, bf16[3072,512]{1,0:T(8,128)(2,1)} %get-tuple-element.99.refs_3_, ...), custom_call_target="tpu_custom_call" | custom-call | flops 9512681472 | bytes 15925248 | tf_op jit(solution)/shard_map/pallas_call | solution.py:57
  398.5 4.0 constant_dynamic-slice_fusion.2
  402.8 11.6 %shard_map.192 = bf16[3072,768]{1,0:T(8,128)(2,1)} custom-call(s32[8]{0:T(128)} %stack.104.info, bf16[3072,128]{1,0:T(8,128)(2,1)} %get-tuple-element.79.refs_0_, bf16[3072,128]{1,0:T(8,128)(2,1)} %get-tuple-element.81.refs_1_, bf16[3072,128]{1,0:T(8,128)(2,1)} %get-tuple-element.83.refs_2_, bf16[3072,512]{1,0:T(8,128)(2,1)} %get-tuple-element.87.refs_3_, ...), custom_call_target="tpu_custom_call" | custom-call | flops 6794772480 | bytes 12386304 | tf_op jit(solution)/shard_map/pallas_call | solution.py:57
  416.1 4.7 constant_dynamic-slice_fusion.3
  424.7 3.1 shard_map.201
  427.8 5.1 collective-permute-start.50
  433.7 3.1 shard_map.200
  436.8 3.3 shard_map.199
  446.0 3.9 collective-permute-done.38
  450.4 4.6 collective-permute-done.34
  455.5 4.6 collective-permute-done.30
  461.8 5.8 collective-permute-done.39
  467.6 6.7 %collective-permute-done.35 = bf16[288,128]{1,0:T(8,128)(2,1)S(1)} collective-permute-done((bf16[288,128]{1,0:T(8,128)(2,1)S(1)}, bf16[288,128]{1,0:T(8,128)(2,1)S(1)}, u32[]{:S(2)}, u32[]{:S(2)}) %collective-permute-start.35) | collective-permute-done | bytes 73760 | tf_op jit(solution)/shard_map/ppermute | solution.py:591
  474.3 5.2 collective-permute-done.31
  479.5 4.5 collective-permute-start.40
  484.1 2.5 collective-permute-done.40
  488.9 2.3 collective-permute-done.36
  493.2 2.3 collective-permute-done.32
  499.6 10.5 %collective-permute-done.51 = bf16[2,432,256]{2,1,0:T(8,128)(2,1)S(1)} collective-permute-done((bf16[2,432,256]{2,1,0:T(8,128)(2,1)S(1)}, bf16[2,432,256]{2,1,0:T(8,128)(2,1)S(1)}, u32[]{:S(2)}, u32[]{:S(2)}) %collective-permute-start.51) | collective-permute-done | bytes 442400 | tf_op jit(solution)/shard_map/ppermute | solution.py:591
  510.1 9.4 %collective-permute-done.47 = bf16[2,432,256]{2,1,0:T(8,128)(2,1)S(1)} collective-permute-done((bf16[2,432,256]{2,1,0:T(8,128)(2,1)S(1)}, bf16[2,432,256]{2,1,0:T(8,128)(2,1)S(1)}, u32[]{:S(2)}, u32[]{:S(2)}) %collective-permute-start.47) | collective-permute-done | bytes 442400 | tf_op jit(solution)/shard_map/ppermute | solution.py:591
  520.1 12.7 %collective-permute-done.43 = bf16[2,432,256]{2,1,0:T(8,128)(2,1)S(1)} collective-permute-done((bf16[2,432,256]{2,1,0:T(8,128)(2,1)S(1)}, bf16[2,432,256]{2,1,0:T(8,128)(2,1)S(1)}, u32[]{:S(2)}, u32[]{:S(2)}) %collective-permute-start.43) | collective-permute-done | bytes 442400 | tf_op jit(solution)/shard_map/ppermute | solution.py:591
  533.0 2.9 collective-permute-start.44
  536.0 13.2 %collective-permute-done.48 = bf16[432,256]{1,0:T(8,128)(2,1)S(1)} collective-permute-done((bf16[432,256]{1,0:T(8,128)(2,1)S(1)}, bf16[432,256]{1,0:T(8,128)(2,1)S(1)}, u32[]{:S(2)}, u32[]{:S(2)}) %collective-permute-start.48) | collective-permute-done | bytes 221216 | tf_op jit(solution)/shard_map/ppermute | solution.py:591
  551.3 2.5 collective-permute-done.44
  558.5 3.5 collective-permute-done.49
  562.1 4.0 collective-permute-done.45
  566.8 11.8 %shard_map.195 = bf16[1416,768]{1,0:T(8,128)(2,1)} custom-call(s32[1416,1]{1,0:T(8,128)} %fusion.12.dst, bf16[1456,768]{1,0:T(8,128)(2,1)} %get-tuple-element.74.x, bf16[1456,768]{1,0:T(8,128)(2,1)} %get-tuple-element.146.a, bf16[1456,768]{1,0:T(8,128)(2,1)} %collective-permute-done.28.b, bf16[1456,768]{1,0:T(8,128)(2,1)} %get-tuple-element.76.cot, ...), custom_call_target="tpu_custom_call" | custom-call | flops 4000000000 | bytes 12000000 | tf_op jit(solution)/shard_map/pallas_call | solution.py:57
  579.3 8.7 %shard_map.193 = bf16[1416,768]{1,0:T(8,128)(2,1)} custom-call(s32[1416,1]{1,0:T(8,128)} %fusion.12.dst, bf16[1456,768]{1,0:T(8,128)(2,1)} %get-tuple-element.74.x, bf16[1456,768]{1,0:T(8,128)(2,1)} %get-tuple-element.148.a, bf16[1456,768]{1,0:T(8,128)(2,1)} %collective-permute-done.27.b, f32[1,768]{1,0:T(1,128)} %reshape.397.bias), custom_call_target="tpu_custom_call" | custom-call | flops 4000000000 | bytes 12000000 | tf_op jit(solution)/shard_map/pallas_call | solution.py:57
  589.5 5.4 shard_map.202
  (302 shorter events, 90.6 us)
Async XLA Ops:
  4.2 24.3 %collective-permute-start = (bf16[5,128]{1,0:T(8,128)(2,1)S(1)}, bf16[5,128]{1,0:T(8,128)(2,1)S(1)}, u32[]{:S(2)}, u32[]{:S(2)}) collective-permute-start(bf16[5,128]{1,0:T(8,128)(2,1)S(1)} %bitcast.128), channel_id=1, source_target_pairs={{0,4},{1,5},{2,6},{3,7},{4,0},{5,1},{6,2},{7,3},{8,12},{9,13},{10,... | collective-permute-start | bytes 3848 | tf_op jit(solution)/shard_map/ppermute | solution.py:591
  11.6 53.3 %collective-permute-start.5 = (bf16[288,128]{1,0:T(8,128)(2,1)}, bf16[288,128]{1,0:T(8,128)(2,1)S(1)}, u32[]{:S(2)}, u32[]{:S(2)}) collective-permute-start(bf16[288,128]{1,0:T(8,128)(2,1)} %get-tuple-element.77), channel_id=1, source_target_pairs={{0,4},{1,5},{2,6},{3,7},{4,0},{5,1},{6,2},{7,3},{8,12},{9,13},{10,... | collective-permute-start | bytes 221192 | tf_op jit(solution)/shard_map/ppermute | solution.py:591
  11.6 57.6 %collective-permute-start.12 = (bf16[288,128]{1,0:T(8,128)(2,1)}, bf16[288,128]{1,0:T(8,128)(2,1)S(1)}, u32[]{:S(2)}, u32[]{:S(2)}) collective-permute-start(bf16[288,128]{1,0:T(8,128)(2,1)} %get-tuple-element.80), channel_id=1, source_target_pairs={{0,4},{1,5},{2,6},{3,7},{4,0},{5,1},{6,2},{7,3},{8,12},{9,13},{10,... | collective-permute-start | bytes 221192 | tf_op jit(solution)/shard_map/ppermute | solution.py:591
  14.5 51.2 %collective-permute-start.15 = (bf16[288,128]{1,0:T(8,128)(2,1)}, bf16[288,128]{1,0:T(8,128)(2,1)S(1)}, u32[]{:S(2)}, u32[]{:S(2)}) collective-permute-start(bf16[288,128]{1,0:T(8,128)(2,1)} %get-tuple-element.82), channel_id=1, source_target_pairs={{0,4},{1,5},{2,6},{3,7},{4,0},{5,1},{6,2},{7,3},{8,12},{9,13},{10,... | collective-permute-start | bytes 221192 | tf_op jit(solution)/shard_map/ppermute | solution.py:591
  14.5 78.7 %collective-permute-start.18 = (bf16[432,256]{1,0:T(8,128)(2,1)}, bf16[432,256]{1,0:T(8,128)(2,1)S(1)}, u32[]{:S(2)}, u32[]{:S(2)}) collective-permute-start(bf16[432,256]{1,0:T(8,128)(2,1)} %get-tuple-element.84), channel_id=1, source_target_pairs={{0,4},{1,5},{2,6},{3,7},{4,0},{5,1},{6,2},{7,3},{8,12},{9,13},{10,... | collective-permute-start | bytes 663560 | tf_op jit(solution)/shard_map/ppermute | solution.py:591
  28.5 4.0 collective-permute-start.1
  32.5 7.4 %collective-permute-start.2 = (bf16[4,5,128]{2,1,0:T(8,128)(2,1)S(1)}, bf16[4,5,128]{2,1,0:T(8,128)(2,1)S(1)}, u32[]{:S(2)}, u32[]{:S(2)}) collective-permute-start(bf16[4,5,128]{2,1,0:T(8,128)(2,1)S(1)} %pad_maximum_fusion.17), channel_id=1, source_target_pairs={{0,1},{1,0},{2,3},{3,2},{4,5},{5,4},{6,7},{7,6},{8,9},{9,8},{10,11... | collective-permute-start | bytes 15368 | tf_op jit(solution)/shard_map/ppermute | solution.py:591
  39.9 25.0 %collective-permute-start.8 = (bf16[480,384]{1,0:T(8,128)(2,1)}, bf16[480,384]{1,0:T(8,128)(2,1)S(1)}, u32[]{:S(2)}, u32[]{:S(2)}) collective-permute-start(bf16[480,384]{1,0:T(8,128)(2,1)} %get-tuple-element.78), channel_id=1, source_target_pairs={{0,4},{1,5},{8,12},{9,13},{16,20},{17,21},{24,28},{25,29}} | collective-permute-start | bytes 1105928 | tf_op jit(solution)/shard_map/ppermute | solution.py:591
  64.8 28.5 %collective-permute-start.21 = (bf16[432,256]{1,0:T(8,128)(2,1)S(1)}, bf16[432,256]{1,0:T(8,128)(2,1)S(1)}, u32[]{:S(2)}, u32[]{:S(2)}) collective-permute-start(bf16[432,256]{1,0:T(8,128)(2,1)S(1)} %copy-done.12), channel_id=1, source_target_pairs={{0,4},{1,5},{2,6},{3,7},{4,0},{5,1},{6,2},{7,3},{8,12},{9,13},{10,... | collective-permute-start | bytes 663560 | tf_op jit(solution)/shard_map/ppermute | solution.py:591
  64.9 9.0 %collective-permute-start.6 = (bf16[2,288,128]{2,1,0:T(8,128)(2,1)S(1)}, bf16[2,288,128]{2,1,0:T(8,128)(2,1)S(1)}, u32[]{:S(2)}, u32[]{:S(2)}) collective-permute-start(bf16[2,288,128]{2,1,0:T(8,128)(2,1)S(1)} %pad_maximum_fusion.14), channel_id=1, source_target_pairs={{0,2},{1,3},{2,0},{3,1},{4,6},{5,7},{6,4},{7,5},{8,10},{9,11},{10,... | collective-permute-start | bytes 442376 | tf_op jit(solution)/shard_map/ppermute | solution.py:591
  65.7 18.1 %collective-permute-start.9 = (bf16[480,384]{1,0:T(8,128)(2,1)S(1)}, bf16[480,384]{1,0:T(8,128)(2,1)S(1)}, u32[]{:S(2)}, u32[]{:S(2)}) collective-permute-start(bf16[480,384]{1,0:T(8,128)(2,1)S(1)} %broadcast_select_fusion), channel_id=1, source_target_pairs={{0,2},{1,3},{4,6},{5,7},{8,10},{9,11},{12,14},{13,15},{16,18},{17,... | collective-permute-start | bytes 1105928 | tf_op jit(solution)/shard_map/ppermute | solution.py:591
  69.2 14.5 %collective-permute-start.24 = (bf16[432,256]{1,0:T(8,128)(2,1)S(1)}, bf16[432,256]{1,0:T(8,128)(2,1)S(1)}, u32[]{:S(2)}, u32[]{:S(2)}) collective-permute-start(bf16[432,256]{1,0:T(8,128)(2,1)S(1)} %copy-done.11), channel_id=1, source_target_pairs={{0,4},{1,5},{2,6},{3,7},{4,0},{5,1},{6,2},{7,3},{8,12},{9,13},{10,... | collective-permute-start | bytes 663560 | tf_op jit(solution)/shard_map/ppermute | solution.py:591
  73.9 114.3 %collective-permute-start.3 = (bf16[1456,768]{1,0:T(8,128)(2,1)}, bf16[1456,768]{1,0:T(8,128)(2,1)}, u32[]{:S(2)}, u32[]{:S(2)}) collective-permute-start(bf16[1456,768]{1,0:T(8,128)(2,1)} %get-tuple-element.75), channel_id=1, source_target_pairs={{0,8},{1,9},{2,10},{3,11},{4,12},{5,13},{6,14},{7,15},{8,0},{9,1},... | collective-permute-start | bytes 6709256 | tf_op jit(solution)/shard_map/ppermute | solution.py:591
  83.7 7.8 %collective-permute-start.13 = (bf16[2,288,128]{2,1,0:T(8,128)(2,1)S(1)}, bf16[2,288,128]{2,1,0:T(8,128)(2,1)S(1)}, u32[]{:S(2)}, u32[]{:S(2)}) collective-permute-start(bf16[2,288,128]{2,1,0:T(8,128)(2,1)S(1)} %pad_maximum_fusion.15), channel_id=1, source_target_pairs={{0,2},{1,3},{2,0},{3,1},{4,6},{5,7},{6,4},{7,5},{8,10},{9,11},{10,... | collective-permute-start | bytes 442376 | tf_op jit(solution)/shard_map/ppermute | solution.py:591
  83.8 7.2 %collective-permute-start.16 = (bf16[2,288,128]{2,1,0:T(8,128)(2,1)S(1)}, bf16[2,288,128]{2,1,0:T(8,128)(2,1)S(1)}, u32[]{:S(2)}, u32[]{:S(2)}) collective-permute-start(bf16[2,288,128]{2,1,0:T(8,128)(2,1)S(1)} %pad_maximum_fusion.16), channel_id=1, source_target_pairs={{0,2},{1,3},{2,0},{3,1},{4,6},{5,7},{6,4},{7,5},{8,10},{9,11},{10,... | collective-permute-start | bytes 442376 | tf_op jit(solution)/shard_map/ppermute | solution.py:591
  91.0 15.0 %collective-permute-start.10 = (bf16[480,384]{1,0:T(8,128)(2,1)S(1)}, bf16[480,384]{1,0:T(8,128)(2,1)S(1)}, u32[]{:S(2)}, u32[]{:S(2)}) collective-permute-start(bf16[480,384]{1,0:T(8,128)(2,1)S(1)} %broadcast_select_fusion.1), channel_id=1, source_target_pairs={{0,1},{1,0},{2,3},{3,2},{4,5},{5,4},{6,7},{7,6},{8,9},{9,8},{10,11... | collective-permute-start | bytes 1105928 | tf_op jit(solution)/shard_map/ppermute | solution.py:591
  91.5 13.7 %collective-permute-start.17 = (bf16[4,288,128]{2,1,0:T(8,128)(2,1)S(1)}, bf16[4,288,128]{2,1,0:T(8,128)(2,1)S(1)}, u32[]{:S(2)}, u32[]{:S(2)}) collective-permute-start(bf16[4,288,128]{2,1,0:T(8,128)(2,1)S(1)} %pad_maximum_fusion.10.near), channel_id=1, source_target_pairs={{0,1},{1,0},{2,3},{3,2},{4,5},{5,4},{6,7},{7,6},{8,9},{9,8},{10,11... | collective-permute-start | bytes 884744 | tf_op jit(solution)/shard_map/ppermute | solution.py:591
  93.2 98.2 %collective-permute-start.4 = (bf16[1456,768]{1,0:T(8,128)(2,1)}, bf16[1456,768]{1,0:T(8,128)(2,1)}, u32[]{:S(2)}, u32[]{:S(2)}) collective-permute-start(bf16[1456,768]{1,0:T(8,128)(2,1)} %get-tuple-element.76.cot), channel_id=1, source_target_pairs={{0,8},{1,9},{2,10},{3,11},{4,12},{5,13},{6,14},{7,15},{8,0},{9,1},... | collective-permute-start | bytes 6709256 | tf_op jit(solution)/shard_map/ppermute | solution.py:591
  93.3 15.7 %collective-permute-start.19 = (bf16[2,432,256]{2,1,0:T(8,128)(2,1)S(1)}, bf16[2,432,256]{2,1,0:T(8,128)(2,1)S(1)}, u32[]{:S(2)}, u32[]{:S(2)}) collective-permute-start(bf16[2,432,256]{2,1,0:T(8,128)(2,1)S(1)} %pad_maximum_fusion.5), channel_id=1, source_target_pairs={{0,2},{1,3},{2,0},{3,1},{4,6},{5,7},{6,4},{7,5},{8,10},{9,11},{10,... | collective-permute-start | bytes 1327112 | tf_op jit(solution)/shard_map/ppermute | solution.py:591
  105.2 13.1 %collective-permute-start.22 = (bf16[2,432,256]{2,1,0:T(8,128)(2,1)S(1)}, bf16[2,432,256]{2,1,0:T(8,128)(2,1)S(1)}, u32[]{:S(2)}, u32[]{:S(2)}) collective-permute-start(bf16[2,432,256]{2,1,0:T(8,128)(2,1)S(1)} %pad_maximum_fusion.6), channel_id=1, source_target_pairs={{0,2},{1,3},{2,0},{3,1},{4,6},{5,7},{6,4},{7,5},{8,10},{9,11},{10,... | collective-permute-start | bytes 1327112 | tf_op jit(solution)/shard_map/ppermute | solution.py:591
  106.0 18.9 %collective-permute-start.25 = (bf16[2,432,256]{2,1,0:T(8,128)(2,1)S(1)}, bf16[2,432,256]{2,1,0:T(8,128)(2,1)S(1)}, u32[]{:S(2)}, u32[]{:S(2)}) collective-permute-start(bf16[2,432,256]{2,1,0:T(8,128)(2,1)S(1)} %pad_maximum_fusion.7), channel_id=1, source_target_pairs={{0,2},{1,3},{2,0},{3,1},{4,6},{5,7},{6,4},{7,5},{8,10},{9,11},{10,... | collective-permute-start | bytes 1327112 | tf_op jit(solution)/shard_map/ppermute | solution.py:591
  109.1 16.2 %collective-permute-start.14 = (bf16[4,288,128]{2,1,0:T(8,128)(2,1)S(1)}, bf16[4,288,128]{2,1,0:T(8,128)(2,1)S(1)}, u32[]{:S(2)}, u32[]{:S(2)}) collective-permute-start(bf16[4,288,128]{2,1,0:T(8,128)(2,1)S(1)} %pad_maximum_fusion.9.near), channel_id=1, source_target_pairs={{0,1},{1,0},{2,3},{3,2},{4,5},{5,4},{6,7},{7,6},{8,9},{9,8},{10,11... | collective-permute-start | bytes 884744 | tf_op jit(solution)/shard_map/ppermute | solution.py:591
  118.3 7.5 %collective-permute-start.7 = (bf16[4,288,128]{2,1,0:T(8,128)(2,1)S(1)}, bf16[4,288,128]{2,1,0:T(8,128)(2,1)S(1)}, u32[]{:S(2)}, u32[]{:S(2)}) collective-permute-start(bf16[4,288,128]{2,1,0:T(8,128)(2,1)S(1)} %pad_maximum_fusion.8.near), channel_id=1, source_target_pairs={{0,1},{1,0},{2,3},{3,2},{4,5},{5,4},{6,7},{7,6},{8,9},{9,8},{10,11... | collective-permute-start | bytes 884744 | tf_op jit(solution)/shard_map/ppermute | solution.py:591
  125.3 22.6 %collective-permute-start.26 = (bf16[4,432,256]{2,1,0:T(8,128)(2,1)S(1)}, bf16[4,432,256]{2,1,0:T(8,128)(2,1)}, u32[]{:S(2)}, u32[]{:S(2)}) collective-permute-start(bf16[4,432,256]{2,1,0:T(8,128)(2,1)S(1)} %pad_maximum_fusion.2.near), channel_id=1, source_target_pairs={{0,1},{1,0},{2,3},{3,2},{4,5},{5,4},{6,7},{7,6},{8,9},{9,8},{10,11... | collective-permute-start | bytes 2654216 | tf_op jit(solution)/shard_map/ppermute | solution.py:591
  125.9 41.0 %collective-permute-start.23 = (bf16[4,432,256]{2,1,0:T(8,128)(2,1)S(1)}, bf16[4,432,256]{2,1,0:T(8,128)(2,1)}, u32[]{:S(2)}, u32[]{:S(2)}) collective-permute-start(bf16[4,432,256]{2,1,0:T(8,128)(2,1)S(1)} %pad_maximum_fusion.1.near), channel_id=1, source_target_pairs={{0,1},{1,0},{2,3},{3,2},{4,5},{5,4},{6,7},{7,6},{8,9},{9,8},{10,11... | collective-permute-start | bytes 2654216 | tf_op jit(solution)/shard_map/ppermute | solution.py:591
  127.4 58.0 %collective-permute-start.20 = (bf16[4,432,256]{2,1,0:T(8,128)(2,1)S(1)}, bf16[4,432,256]{2,1,0:T(8,128)(2,1)}, u32[]{:S(2)}, u32[]{:S(2)}) collective-permute-start(bf16[4,432,256]{2,1,0:T(8,128)(2,1)S(1)} %pad_maximum_fusion.near), channel_id=1, source_target_pairs={{0,1},{1,0},{2,3},{3,2},{4,5},{5,4},{6,7},{7,6},{8,9},{9,8},{10,11... | collective-permute-start | bytes 2654216 | tf_op jit(solution)/shard_map/ppermute | solution.py:591
  218.2 221.9 %collective-permute-start.37 = (bf16[4,288,128]{2,1,0:T(8,128)(2,1)}, bf16[4,288,128]{2,1,0:T(8,128)(2,1)}, u32[]{:S(2)}, u32[]{:S(2)}) collective-permute-start(bf16[4,288,128]{2,1,0:T(8,128)(2,1)} %get-tuple-element.110), channel_id=1, source_target_pairs={{0,1},{1,0},{2,3},{3,2},{4,5},{5,4},{6,7},{7,6},{8,9},{9,8},{10,11... | collective-permute-start | bytes 884744 | tf_op jit(solution)/shard_map/ppermute | solution.py:591
  244.0 197.3 %collective-permute-start.33 = (bf16[4,288,128]{2,1,0:T(8,128)(2,1)}, bf16[4,288,128]{2,1,0:T(8,128)(2,1)}, u32[]{:S(2)}, u32[]{:S(2)}) collective-permute-start(bf16[4,288,128]{2,1,0:T(8,128)(2,1)} %get-tuple-element.107), channel_id=1, source_target_pairs={{0,1},{1,0},{2,3},{3,2},{4,5},{5,4},{6,7},{7,6},{8,9},{9,8},{10,11... | collective-permute-start | bytes 884744 | tf_op jit(solution)/shard_map/ppermute | solution.py:591
  302.4 5.8 collective-permute-start.60
  302.8 121.0 %collective-permute-start.41 = (bf16[144,768]{1,0:T(8,128)(2,1)S(1)}, bf16[144,768]{1,0:T(8,128)(2,1)S(1)}, u32[]{:S(2)}, u32[]{:S(2)}) collective-permute-start(bf16[144,768]{1,0:T(8,128)(2,1)S(1)} %fusion.36), channel_id=1, source_target_pairs={{0,8},{1,9},{2,10},{3,11},{4,12},{5,13},{6,14},{7,15},{8,0},{9,1},... | collective-permute-start | bytes 663560 | tf_op jit(solution)/shard_map/ppermute | solution.py:591
  306.4 138.0 %collective-permute-start.29 = (bf16[4,288,128]{2,1,0:T(8,128)(2,1)}, bf16[4,288,128]{2,1,0:T(8,128)(2,1)}, u32[]{:S(2)}, u32[]{:S(2)}) collective-permute-start(bf16[4,288,128]{2,1,0:T(8,128)(2,1)} %get-tuple-element.104), channel_id=1, source_target_pairs={{0,1},{1,0},{2,3},{3,2},{4,5},{5,4},{6,7},{7,6},{8,9},{9,8},{10,11... | collective-permute-start | bytes 884744 | tf_op jit(solution)/shard_map/ppermute | solution.py:591
  308.2 88.2 %collective-permute-start.61 = (f32[32,128]{1,0:T(8,128)S(1)}, f32[32,128]{1,0:T(8,128)S(1)}, u32[]{:S(2)}, u32[]{:S(2)}) collective-permute-start(f32[32,128]{1,0:T(8,128)S(1)} %add.387), channel_id=1, source_target_pairs={{0,16},{1,17},{2,18},{3,19},{4,20},{5,21},{6,22},{7,23},{8,24},{9,... | collective-permute-start | bytes 49160 | tf_op jit(solution)/shard_map/ppermute | solution.py:591
  396.4 6.1 %collective-permute-start.62 = (f32[32,128]{1,0:T(8,128)S(1)}, f32[32,128]{1,0:T(8,128)S(1)}, u32[]{:S(2)}, u32[]{:S(2)}) collective-permute-start(f32[32,128]{1,0:T(8,128)S(1)} %add.388), channel_id=1, source_target_pairs={{0,1},{1,0},{2,3},{3,2},{4,5},{5,4},{6,7},{7,6},{8,9},{9,8},{10,11... | collective-permute-start | bytes 49160 | tf_op jit(solution)/shard_map/ppermute | solution.py:591
  402.6 11.9 %collective-permute-start.63 = (f32[32,128]{1,0:T(8,128)S(1)}, f32[32,128]{1,0:T(8,128)S(1)}, u32[]{:S(2)}, u32[]{:S(2)}) collective-permute-start(f32[32,128]{1,0:T(8,128)S(1)} %add.389), channel_id=1, source_target_pairs={{0,2},{1,3},{2,0},{3,1},{4,6},{5,7},{6,4},{7,5},{8,10},{9,11},{10,... | collective-permute-start | bytes 49160 | tf_op jit(solution)/shard_map/ppermute | solution.py:591
  414.5 6.3 %collective-permute-start.64 = (f32[32,128]{1,0:T(8,128)S(1)}, f32[32,128]{1,0:T(8,128)S(1)}, u32[]{:S(2)}, u32[]{:S(2)}) collective-permute-start(f32[32,128]{1,0:T(8,128)S(1)} %add.390), channel_id=1, source_target_pairs={{0,4},{1,5},{2,6},{3,7},{4,0},{5,1},{6,2},{7,3},{8,12},{9,13},{10,... | collective-permute-start | bytes 49160 | tf_op jit(solution)/shard_map/ppermute | solution.py:591
  420.8 145.4 %collective-permute-start.28 = (bf16[1456,768]{1,0:T(8,128)(2,1)S(1)}, bf16[1456,768]{1,0:T(8,128)(2,1)}, u32[]{:S(2)}, u32[]{:S(2)}) collective-permute-start(bf16[1456,768]{1,0:T(8,128)(2,1)S(1)} %get-tuple-element.145), channel_id=1, source_target_pairs={{0,8},{1,9},{2,10},{3,11},{4,12},{5,13},{6,14},{7,15},{8,0},{9,1},... | collective-permute-start | bytes 6709256 | tf_op jit(solution)/shard_map/ppermute | solution.py:591
  427.8 68.4 %collective-permute-start.50 = (bf16[4,432,256]{2,1,0:T(8,128)(2,1)}, bf16[4,432,256]{2,1,0:T(8,128)(2,1)S(1)}, u32[]{:S(2)}, u32[]{:S(2)}) collective-permute-start(bf16[4,432,256]{2,1,0:T(8,128)(2,1)} %get-tuple-element.125), channel_id=1, source_target_pairs={{0,1},{1,0},{2,3},{3,2},{4,5},{5,4},{6,7},{7,6},{8,9},{9,8},{10,11... | collective-permute-start | bytes 2654216 | tf_op jit(solution)/shard_map/ppermute | solution.py:591
  440.1 56.8 %collective-permute-start.46 = (bf16[4,432,256]{2,1,0:T(8,128)(2,1)}, bf16[4,432,256]{2,1,0:T(8,128)(2,1)S(1)}, u32[]{:S(2)}, u32[]{:S(2)}) collective-permute-start(bf16[4,432,256]{2,1,0:T(8,128)(2,1)} %get-tuple-element.121), channel_id=1, source_target_pairs={{0,1},{1,0},{2,3},{3,2},{4,5},{5,4},{6,7},{7,6},{8,9},{9,8},{10,11... | collective-permute-start | bytes 2654216 | tf_op jit(solution)/shard_map/ppermute | solution.py:591
  441.3 56.0 %collective-permute-start.42 = (bf16[4,432,256]{2,1,0:T(8,128)(2,1)}, bf16[4,432,256]{2,1,0:T(8,128)(2,1)S(1)}, u32[]{:S(2)}, u32[]{:S(2)}) collective-permute-start(bf16[4,432,256]{2,1,0:T(8,128)(2,1)} %get-tuple-element.117), channel_id=1, source_target_pairs={{0,1},{1,0},{2,3},{3,2},{4,5},{5,4},{6,7},{7,6},{8,9},{9,8},{10,11... | collective-permute-start | bytes 2654216 | tf_op jit(solution)/shard_map/ppermute | solution.py:591
  444.4 5.5 collective-permute-start.38
  449.9 5.1 collective-permute-start.34
  455.0 5.1 collective-permute-start.30
  460.2 7.4 %collective-permute-start.39 = (bf16[288,128]{1,0:T(8,128)(2,1)S(1)}, bf16[288,128]{1,0:T(8,128)(2,1)S(1)}, u32[]{:S(2)}, u32[]{:S(2)}) collective-permute-start(bf16[288,128]{1,0:T(8,128)(2,1)S(1)} %fusion.46), channel_id=1, source_target_pairs={{0,4},{1,5},{2,6},{3,7},{4,0},{5,1},{6,2},{7,3},{8,12},{9,13},{10,... | collective-permute-start | bytes 221192 | tf_op jit(solution)/shard_map/ppermute | solution.py:591
  467.5 6.7 %collective-permute-start.35 = (bf16[288,128]{1,0:T(8,128)(2,1)S(1)}, bf16[288,128]{1,0:T(8,128)(2,1)S(1)}, u32[]{:S(2)}, u32[]{:S(2)}) collective-permute-start(bf16[288,128]{1,0:T(8,128)(2,1)S(1)} %fusion.44), channel_id=1, source_target_pairs={{0,4},{1,5},{2,6},{3,7},{4,0},{5,1},{6,2},{7,3},{8,12},{9,13},{10,... | collective-permute-start | bytes 221192 | tf_op jit(solution)/shard_map/ppermute | solution.py:591
  474.3 5.3 collective-permute-start.31
  479.5 7.1 %collective-permute-start.40 = (bf16[288,128]{1,0:T(8,128)(2,1)S(1)}, bf16[288,128]{1,0:T(8,128)(2,1)S(1)}, u32[]{:S(2)}, u32[]{:S(2)}) collective-permute-start(bf16[288,128]{1,0:T(8,128)(2,1)S(1)} %fusion.38), channel_id=1, source_target_pairs={{0,16},{1,17},{2,18},{3,19},{4,20},{5,21},{6,22},{7,23},{8,24},{9,... | collective-permute-start | bytes 221192 | tf_op jit(solution)/shard_map/ppermute | solution.py:591
  486.6 4.6 collective-permute-start.36
  491.2 4.4 collective-permute-start.32
  495.5 83.3 %collective-permute-start.27 = (bf16[1456,768]{1,0:T(8,128)(2,1)}, bf16[1456,768]{1,0:T(8,128)(2,1)}, u32[]{:S(2)}, u32[]{:S(2)}) collective-permute-start(bf16[1456,768]{1,0:T(8,128)(2,1)} %get-tuple-element.147), channel_id=1, source_target_pairs={{0,8},{1,9},{2,10},{3,11},{4,12},{5,13},{6,14},{7,15},{8,0},{9,1},... | collective-permute-start | bytes 6709256 | tf_op jit(solution)/shard_map/ppermute | solution.py:591
  496.2 82.4 %collective-permute-start.56 = (f32[288,128]{1,0:T(8,128)S(1)}, f32[288,128]{1,0:T(8,128)}, u32[]{:S(2)}, u32[]{:S(2)}) collective-permute-start(f32[288,128]{1,0:T(8,128)S(1)} %convert_add_fusion.9.refs_2_), channel_id=1, source_target_pairs={{0,8},{1,9},{2,10},{3,11},{4,12},{5,13},{6,14},{7,15},{8,0},{9,1},... | collective-permute-start | bytes 442376 | tf_op jit(solution)/shard_map/ppermute | solution.py:591
  496.9 13.1 %collective-permute-start.51 = (bf16[2,432,256]{2,1,0:T(8,128)(2,1)S(1)}, bf16[2,432,256]{2,1,0:T(8,128)(2,1)S(1)}, u32[]{:S(2)}, u32[]{:S(2)}) collective-permute-start(bf16[2,432,256]{2,1,0:T(8,128)(2,1)S(1)} %get-tuple-element.150), channel_id=1, source_target_pairs={{0,2},{1,3},{2,0},{3,1},{4,6},{5,7},{6,4},{7,5},{8,10},{9,11},{10,... | collective-permute-start | bytes 1327112 | tf_op jit(solution)/shard_map/ppermute | solution.py:591
  497.3 22.2 %collective-permute-start.47 = (bf16[2,432,256]{2,1,0:T(8,128)(2,1)S(1)}, bf16[2,432,256]{2,1,0:T(8,128)(2,1)S(1)}, u32[]{:S(2)}, u32[]{:S(2)}) collective-permute-start(bf16[2,432,256]{2,1,0:T(8,128)(2,1)S(1)} %get-tuple-element.152), channel_id=1, source_target_pairs={{0,2},{1,3},{2,0},{3,1},{4,6},{5,7},{6,4},{7,5},{8,10},{9,11},{10,... | collective-permute-start | bytes 1327112 | tf_op jit(solution)/shard_map/ppermute | solution.py:591
  510.0 22.8 %collective-permute-start.43 = (bf16[2,432,256]{2,1,0:T(8,128)(2,1)S(1)}, bf16[2,432,256]{2,1,0:T(8,128)(2,1)S(1)}, u32[]{:S(2)}, u32[]{:S(2)}) collective-permute-start(bf16[2,432,256]{2,1,0:T(8,128)(2,1)S(1)} %get-tuple-element.154), channel_id=1, source_target_pairs={{0,2},{1,3},{2,0},{3,1},{4,6},{5,7},{6,4},{7,5},{8,10},{9,11},{10,... | collective-permute-start | bytes 1327112 | tf_op jit(solution)/shard_map/ppermute | solution.py:591
  519.5 13.5 %collective-permute-start.52 = (bf16[432,256]{1,0:T(8,128)(2,1)S(1)}, bf16[432,256]{1,0:T(8,128)(2,1)S(1)}, u32[]{:S(2)}, u32[]{:S(2)}) collective-permute-start(bf16[432,256]{1,0:T(8,128)(2,1)S(1)} %fusion.35), channel_id=1, source_target_pairs={{0,4},{1,5},{2,6},{3,7},{4,0},{5,1},{6,2},{7,3},{8,12},{9,13},{10,... | collective-permute-start | bytes 663560 | tf_op jit(solution)/shard_map/ppermute | solution.py:591
  532.8 16.4 %collective-permute-start.48 = (bf16[432,256]{1,0:T(8,128)(2,1)S(1)}, bf16[432,256]{1,0:T(8,128)(2,1)S(1)}, u32[]{:S(2)}, u32[]{:S(2)}) collective-permute-start(bf16[432,256]{1,0:T(8,128)(2,1)S(1)} %fusion.33), channel_id=1, source_target_pairs={{0,4},{1,5},{2,6},{3,7},{4,0},{5,1},{6,2},{7,3},{8,12},{9,13},{10,... | collective-permute-start | bytes 663560 | tf_op jit(solution)/shard_map/ppermute | solution.py:591
  533.0 20.8 %collective-permute-start.44 = (bf16[432,256]{1,0:T(8,128)(2,1)S(1)}, bf16[432,256]{1,0:T(8,128)(2,1)S(1)}, u32[]{:S(2)}, u32[]{:S(2)}) collective-permute-start(bf16[432,256]{1,0:T(8,128)(2,1)S(1)} %fusion.31), channel_id=1, source_target_pairs={{0,4},{1,5},{2,6},{3,7},{4,0},{5,1},{6,2},{7,3},{8,12},{9,13},{10,... | collective-permute-start | bytes 663560 | tf_op jit(solution)/shard_map/ppermute | solution.py:591
  549.2 7.5 %collective-permute-start.53 = (bf16[432,256]{1,0:T(8,128)(2,1)S(1)}, bf16[432,256]{1,0:T(8,128)(2,1)S(1)}, u32[]{:S(2)}, u32[]{:S(2)}) collective-permute-start(bf16[432,256]{1,0:T(8,128)(2,1)S(1)} %fusion.25), channel_id=1, source_target_pairs={{0,16},{1,17},{2,18},{3,19},{4,20},{5,21},{6,22},{7,23},{8,24},{9,... | collective-permute-start | bytes 663560 | tf_op jit(solution)/shard_map/ppermute | solution.py:591
  553.8 8.2 %collective-permute-start.49 = (bf16[432,256]{1,0:T(8,128)(2,1)S(1)}, bf16[432,256]{1,0:T(8,128)(2,1)S(1)}, u32[]{:S(2)}, u32[]{:S(2)}) collective-permute-start(bf16[432,256]{1,0:T(8,128)(2,1)S(1)} %fusion.26), channel_id=1, source_target_pairs={{0,16},{1,17},{2,18},{3,19},{4,20},{5,21},{6,22},{7,23},{8,24},{9,... | collective-permute-start | bytes 663560 | tf_op jit(solution)/shard_map/ppermute | solution.py:591
  556.7 9.5 %collective-permute-start.45 = (bf16[432,256]{1,0:T(8,128)(2,1)S(1)}, bf16[432,256]{1,0:T(8,128)(2,1)S(1)}, u32[]{:S(2)}, u32[]{:S(2)}) collective-permute-start(bf16[432,256]{1,0:T(8,128)(2,1)S(1)} %fusion.27), channel_id=1, source_target_pairs={{0,16},{1,17},{2,18},{3,19},{4,20},{5,21},{6,22},{7,23},{8,24},{9,... | collective-permute-start | bytes 663560 | tf_op jit(solution)/shard_map/ppermute | solution.py:591
  562.1 25.9 %collective-permute-start.59 = (f32[432,256]{1,0:T(8,128)S(1)}, f32[432,256]{1,0:T(8,128)}, u32[]{:S(2)}, u32[]{:S(2)}) collective-permute-start(f32[432,256]{1,0:T(8,128)S(1)} %convert_add_fusion.3.refs_5_), channel_id=1, source_target_pairs={{0,8},{1,9},{2,10},{3,11},{4,12},{5,13},{6,14},{7,15},{8,0},{9,1},... | collective-permute-start | bytes 1327112 | tf_op jit(solution)/shard_map/ppermute | solution.py:591
  566.2 21.8 %collective-permute-start.58 = (f32[432,256]{1,0:T(8,128)S(1)}, f32[432,256]{1,0:T(8,128)}, u32[]{:S(2)}, u32[]{:S(2)}) collective-permute-start(f32[432,256]{1,0:T(8,128)S(1)} %convert_add_fusion.4.refs_4_), channel_id=1, source_target_pairs={{0,8},{1,9},{2,10},{3,11},{4,12},{5,13},{6,14},{7,15},{8,0},{9,1},... | collective-permute-start | bytes 1327112 | tf_op jit(solution)/shard_map/ppermute | solution.py:591
  566.3 21.8 %collective-permute-start.57 = (f32[432,256]{1,0:T(8,128)S(1)}, f32[432,256]{1,0:T(8,128)S(1)}, u32[]{:S(2)}, u32[]{:S(2)}) collective-permute-start(f32[432,256]{1,0:T(8,128)S(1)} %convert_add_fusion.5.refs_3_), channel_id=1, source_target_pairs={{0,8},{1,9},{2,10},{3,11},{4,12},{5,13},{6,14},{7,15},{8,0},{9,1},... | collective-permute-start | bytes 1327112 | tf_op jit(solution)/shard_map/ppermute | solution.py:591
  578.7 9.3 %collective-permute-start.55 = (f32[288,128]{1,0:T(8,128)S(1)}, f32[288,128]{1,0:T(8,128)S(1)}, u32[]{:S(2)}, u32[]{:S(2)}) collective-permute-start(f32[288,128]{1,0:T(8,128)S(1)} %convert_add_fusion.10.refs_1_), channel_id=1, source_target_pairs={{0,8},{1,9},{2,10},{3,11},{4,12},{5,13},{6,14},{7,15},{8,0},{9,1},... | collective-permute-start | bytes 442376 | tf_op jit(solution)/shard_map/ppermute | solution.py:591
  578.8 9.2 %collective-permute-start.54 = (f32[288,128]{1,0:T(8,128)S(1)}, f32[288,128]{1,0:T(8,128)S(1)}, u32[]{:S(2)}, u32[]{:S(2)}) collective-permute-start(f32[288,128]{1,0:T(8,128)S(1)} %copy-done.21), channel_id=1, source_target_pairs={{0,8},{1,9},{2,10},{3,11},{4,12},{5,13},{6,14},{7,15},{8,0},{9,1},... | collective-permute-start | bytes 442376 | tf_op jit(solution)/shard_map/ppermute | solution.py:591
  (46 other events, 719.1 us)
